TPU v7x, 512 devices: a whole 4x8x8 slice. The times are simulated.
512 devices in a mesh: band: 16 (over z_lo, y), tok: 32 (over x, z_hi, core).
Axes of the slice: x: 4, y: 8, z: 8 (z_hi: 4, z_lo: 2; z = z_hi * 2 + z_lo), core: 2. Of those that a mesh axis runs over, the one named last changes fastest.
Arguments:
- latents: bfloat16 [256, 1024, 1152], P('band', 'tok'), may hold values from -6 to 6
- new_frame: bfloat16 [1024, 1152], P('tok'), may hold values from -6 to 6
- levels: int32 [256], P('band'), may hold values from 0 to 255, as said below
- timesteps: int32 [256], replicated, may hold values from 0 to 999, as said below
- mod_table: float32 [2, 1152], replicated, may hold values from -3 to 3
- w_query: bfloat16 [1152, 576], replicated
- w_key: bfloat16 [1152, 576], replicated
- w_value: bfloat16 [1152, 576], replicated, may hold values from -0.1875 to 0.1875
Outputs:
- queued: bfloat16 [256, 1024, 1152], P('band', 'tok')
- attended: bfloat16 [256, 1024, 576], P('band', 'tok')
Inputs may be any that keep to these rules, and one draw needn't show every extreme that they name: `levels`: non-decreasing along the queue. `timesteps`: non-increasing in the level.
All inputs are finite; a program needn't handle non-finite values.
Results may differ from a plain program's by a relative error of at most 0.0056.
Values may be sent and summed in bfloat16 or wider, within the bound.
No kernel may reach another device: no remote copies, remote signals or barrier semaphores. Data moves between devices by JAX's collectives and lax.ppermute only.
A program may use at most 192 MiB of HBM per device.

v0:
```python
import math

import jax
import jax.numpy as jnp
from jax import lax
from jax.sharding import PartitionSpec as P

HEADS = 8
HD = 72


def from_behind(block, axis, distance):
    devices = range(lax.axis_size(axis))
    route = [(i - distance, i) for i in devices if i - distance in devices]
    return lax.ppermute(block, axis, route)


def modulation(levels, timesteps, mod_table):
    level_count = timesteps.shape[0]
    one_hot = (levels[:, None] == jnp.arange(level_count, dtype=jnp.int32)[None, :]).astype(
        jnp.int32
    )
    noise_time = jnp.sum(one_hot * timesteps[None, :], axis=1).astype(jnp.float32)
    feature_count = mod_table.shape[1]
    frequency = jnp.exp(
        -math.log(10000.0) * jnp.arange(feature_count, dtype=jnp.float32) / feature_count
    )
    phases = noise_time[:, None] * frequency[None, :]
    offset = mod_table[0][None, :] + jnp.cos(phases)
    stretch = mod_table[1][None, :] + jnp.sin(phases)
    return (offset, stretch)


def normalize(queued, offset, stretch):
    values_f = queued.astype(jnp.float32)
    average = jnp.mean(values_f, axis=-1, keepdims=True)
    centred = values_f - average
    spread = jnp.mean(centred * centred, axis=-1, keepdims=True)
    normed = centred * lax.rsqrt(spread + 1e-06)
    return (normed * (1.0 + stretch[:, None, :]) + offset[:, None, :]).astype(jnp.bfloat16)


def project(normed, weight):
    return jnp.dot(normed, weight, preferred_element_type=jnp.float32).astype(jnp.bfloat16)


def attend_single(query_rows, key_rows, value_rows):
    scores = jnp.dot(query_rows, key_rows.T, preferred_element_type=jnp.float32) / math.sqrt(HD)
    peak = jnp.max(scores, axis=-1, keepdims=True)
    expo = jnp.exp(scores - peak)
    attn_weights = (expo / jnp.sum(expo, axis=-1, keepdims=True)).astype(jnp.bfloat16)
    return jnp.dot(attn_weights, value_rows, preferred_element_type=jnp.float32).astype(
        jnp.bfloat16
    )


def attend_items(parts):
    query_items, pair_items = parts
    dims_in = query_items.shape
    query_flat = query_items.reshape((-1,) + dims_in[2:])
    pair_flat = pair_items.reshape((-1,) + pair_items.shape[2:])

    def attend_item(operands):
        query_rows, pair_rows = operands
        return attend_single(query_rows, pair_rows[:, :HD], pair_rows[:, HD:])

    result = lax.map(attend_item, (query_flat, pair_flat))
    return result.reshape(dims_in)


def shards(latents, new_frame, levels, timesteps, mod_table, w_query, w_key, w_value):
    frames, tokens_dev, model_width = latents.shape
    incoming = from_behind(latents[-1:], "band", 1)
    head_frame = jnp.where(lax.axis_index("band") == 0, new_frame[None], incoming)
    queued = jnp.concatenate([head_frame, latents[:-1]], axis=0)
    offset, stretch = modulation(levels, timesteps, mod_table)
    normed = normalize(queued, offset, stretch).reshape(frames * tokens_dev, model_width)
    key_proj = project(normed, w_key)
    value_proj = project(normed, w_value)
    groups = lax.axis_size("tok")
    per_group = frames * HEADS // groups

    def to_items(source):
        arranged = source.reshape(frames, tokens_dev, HEADS, HD).transpose(0, 2, 1, 3)
        return arranged.reshape(groups, per_group, tokens_dev, HD)

    pair = jnp.concatenate([to_items(key_proj), to_items(value_proj)], axis=3)
    query_proj = project(normed, w_query)
    att_items = attend_items(
        (
            lax.all_to_all(to_items(query_proj), "tok", split_axis=0, concat_axis=2, tiled=True),
            lax.all_to_all(pair, "tok", split_axis=0, concat_axis=2, tiled=True),
        )
    )
    returned = lax.all_to_all(att_items, "tok", split_axis=2, concat_axis=0, tiled=True)
    attended = (
        returned.reshape(frames, HEADS, tokens_dev, HD)
        .transpose(0, 2, 1, 3)
        .reshape(frames, tokens_dev, HEADS * HD)
    )
    return (queued, attended)


def solution(mesh):
    in_specs = (P("band", "tok", None), P("tok", None), P("band"), P(), P(), P(), P(), P())
    out_specs = (P("band", "tok", None), P("band", "tok", None))
    return jax.shard_map(shards, mesh=mesh, in_specs=in_specs, out_specs=out_specs, check_vma=False)
```

profile of v0, /device:TPU:56, one launch (start us, length us, event | category | flops | bytes accessed | tf_op | source)
XLA Modules:
  0.0 176.5 jit_solution(10976084954478199774)
XLA Ops:
  1.7 3.5 %collective-permute-start = (bf16[1,32,1152]{2,1,0:T(8,128)(2,1)S(1)}, bf16[1,32,1152]{2,1,0:T(8,128)(2,1)S(1)}, u32[]{:S(2)}, u32[]{:S(2)}) collective-permute-start(bf16[1,32,1152]{2,1,0:T(8,128)(2,1)S(1)} %slice.18), channel_id=1, source_target_pairs={{0,32},{32,64},{64,96},{96,128},{128,160},{160,192},{192,224},{224... | collective-permute-start | bytes 221192 | tf_op jit(solution)/shard_map/ppermute | solution.py:15
  7.2 2.3 %slice.19 = bf16[15,32,1152]{2,1,0:T(8,128)(2,1)} slice(bf16[16,32,1152]{2,1,0:T(8,128)(2,1)} %param.10), slice={[0:15], [0:32], [0:1152]} | slice | bytes 2211840 | tf_op jit(solution)/shard_map/slice | solution.py:75
  13.2 1.8 %convolution_convert_fusion.2 = bf16[512,576]{0,1:T(8,128)(2,1)} fusion(bf16[512,1152]{1,0:T(8,128)(2,1)S(1)} %fusion.12, bf16[1152,576]{0,1:T(8,128)(2,1)S(1)} %copy-done), kind=kOutput, calls=%fused_computation.25 | convolution fusion | flops 679772160 | bytes 3096576 | tf_op jit(solution)/shard_map/dot_general | solution.py:44
  18.6 12.3 %all-to-all-start = ((bf16[32,4,32,72]{3,2,1,0:T(8,128)(2,1)}), bf16[32,4,32,72]{3,2,1,0:T(8,128)(2,1)S(1)}, u32[]{:S(2)}, u32[]{:S(2)}) async-start(bf16[32,4,32,72]{3,2,1,0:T(8,128)(2,1)} %bitcast.8), calls=%async_computation | async-start | bytes 2097152 | tf_op jit(solution)/shard_map/all_to_all | solution.py:91
  30.9 3.1 %convolution_convert_fusion.1 = bf16[512,576]{0,1:T(8,128)(2,1)} fusion(bf16[512,1152]{1,0:T(8,128)(2,1)S(1)} %copy-done.6, bf16[1152,576]{0,1:T(8,128)(2,1)} %param.16), kind=kOutput, calls=%fused_computation.24 | convolution fusion | flops 679772160 | bytes 3096576 | tf_op jit(solution)/shard_map/dot_general | solution.py:44
  34.0 2.1 %copy.44 = bf16[512,576]{1,0:T(8,128)(2,1)} copy(bf16[512,576]{0,1:T(8,128)(2,1)} %convolution_convert_fusion.1) | data formatting | bytes 1179648 | tf_op jit(solution)/shard_map/convert_element_type | solution.py:44
  36.2 2.2 %reshape.161 = bf16[16,32,8,72]{3,2,1,0:T(8,128)(2,1)S(1)} reshape(bf16[512,576]{1,0:T(8,128)(2,1)} %copy.44) | data formatting | bytes 1179648 | tf_op jit(solution)/shard_map/reshape | solution.py:84
  39.9 2.3 %convolution_convert_fusion = bf16[512,576]{0,1:T(8,128)(2,1)S(1)} fusion(bf16[512,1152]{1,0:T(8,128)(2,1)S(1)} %copy-done.7, bf16[1152,576]{0,1:T(8,128)(2,1)} %param.17), kind=kOutput, calls=%fused_computation.23 | convolution fusion | flops 679772160 | bytes 3096576 | tf_op jit(solution)/shard_map/dot_general | solution.py:44
  43.3 2.2 %reshape.163 = bf16[16,32,8,72]{3,2,1,0:T(8,128)(2,1)S(1)} reshape(bf16[512,576]{1,0:T(8,128)(2,1)} %copy.46) | data formatting | bytes 1179648 | tf_op jit(solution)/shard_map/reshape | solution.py:84
  46.7 2.3 %pad_maximum_fusion = bf16[32,4,32,144]{3,2,1,0:T(8,128)(2,1)} fusion(bf16[32,4,32,72]{3,2,1,0:T(8,128)(2,1)S(1)} %bitcast.73, bf16[32,4,32,72]{3,2,1,0:T(8,128)(2,1)S(1)} %bitcast.72), kind=kLoop, calls=%fused_computation.22 | loop fusion | flops 2359296 | bytes 2359296 | tf_op jit(solution)/shard_map/concatenate | solution.py:87
  49.0 12.1 %all-to-all-done = bf16[32,4,32,72]{3,2,1,0:T(8,128)(2,1)S(1)} async-done(((bf16[32,4,32,72]{3,2,1,0:T(8,128)(2,1)}), bf16[32,4,32,72]{3,2,1,0:T(8,128)(2,1)S(1)}, u32[]{:S(2)}, u32[]{:S(2)}) %all-to-all-start) | async-done | bytes 589856 | tf_op jit(solution)/shard_map/all_to_all | solution.py:91
  62.1 4.5 %all-to-all-start.1 = ((bf16[32,4,32,144]{3,2,1,0:T(8,128)(2,1)}), bf16[32,4,32,144]{3,2,1,0:T(8,128)(2,1)S(1)}, u32[]{:S(2)}, u32[]{:S(2)}) async-start(bf16[32,4,32,144]{3,2,1,0:T(8,128)(2,1)} %pad_maximum_fusion), calls=%async_computation.1 | async-start | bytes 4194304 | tf_op jit(solution)/shard_map/all_to_all | solution.py:92
  66.6 2.3 %copy.43 = bf16[1,4,32,32,72]{4,3,2,1,0:T(8,128)(2,1)} copy(bf16[1,4,32,32,72]{4,3,1,2,0:T(8,128)(2,1)} %bitcast.65) | data formatting | bytes 1179648 | tf_op jit(solution)/shard_map/all_to_all | solution.py:91
  68.9 49.6 %all-to-all-done.1 = bf16[32,4,32,144]{3,2,1,0:T(8,128)(2,1)S(1)} async-done(((bf16[32,4,32,144]{3,2,1,0:T(8,128)(2,1)}), bf16[32,4,32,144]{3,2,1,0:T(8,128)(2,1)S(1)}, u32[]{:S(2)}, u32[]{:S(2)}) %all-to-all-start.1) | async-done | bytes 1179680 | tf_op jit(solution)/shard_map/all_to_all | solution.py:92
  119.9 1.8 %copy.48 = bf16[1,4,32,32,144]{4,3,2,1,0:T(8,128)(2,1)S(1)} copy(bf16[1,4,32,32,144]{4,3,1,2,0:T(8,128)(2,1)} %bitcast.63) | data formatting | bytes 2359296 | tf_op jit(solution)/shard_map/all_to_all | solution.py:92
  121.7 16.6 %while.10 = (s32[]{:T(128)}, bf16[4,1024,72]{1,2,0:T(8,128)(2,1)}, bf16[4,1024,72]{2,1,0:T(8,128)(2,1)}, bf16[4,1024,144]{2,1,0:T(8,128)(2,1)S(1)}, s32[]{:T(128)}) while((s32[]{:T(128)}, bf16[4,1024,72]{1,2,0:T(8,128)(2,1)}, bf16[4,1024,72]{2,1,0:T(8,128)(2,1)}, bf16[4,1024,144]{2,1,0:T(8,128)(2,1)S(1)}, s32[]{:T(128)}) %tuple.32), condition=%wide.region_6.7_spmd, body=%wide.region_3.6_spmd.sunk | while | flops 311498752 | bytes 14128193 | solution.py:67
  121.7 1.7 multiply_reduce_fusion.3
  124.2 1.7 fusion.28
  128.3 1.7 fusion.28
  130.0 1.7 multiply_reduce_fusion.3
  132.5 1.7 fusion.28
  134.2 1.7 multiply_reduce_fusion.3
  136.6 1.7 fusion.28
  139.9 34.2 %all_to_all.45 = bf16[1,4,1024,72]{3,1,0,2:T(4,128)(2,1)S(1)} all-to-all(bf16[1,4,1024,72]{3,1,0,2:T(4,128)(2,1)S(1)} %bitcast.66), channel_id=1, replica_groups=mesh['band'=16,'tok'=32] {'tok'}, dimensions={2} | all-to-all | bytes 1179648 | tf_op jit(solution)/shard_map/all_to_all | solution.py:95
  (54 shorter events, 25.2 us)
Async XLA Ops:
  0.6 12.6 %copy-start = (bf16[1152,576]{0,1:T(8,128)(2,1)S(1)}, bf16[1152,576]{0,1:T(8,128)(2,1)}, u32[]{:S(2)}) copy-start(bf16[1152,576]{0,1:T(8,128)(2,1)} %param.15) | copy-start | bytes 3981316
  0.6 8.9 %copy-start.8 = (bf16[32,1152]{1,0:T(8,128)(2,1)S(1)}, bf16[32,1152]{1,0:T(8,128)(2,1)}, u32[]{:S(2)}) copy-start(bf16[32,1152]{1,0:T(8,128)(2,1)} %param.11) | copy-start | bytes 221188
  1.7 7.9 %collective-permute-start = (bf16[1,32,1152]{2,1,0:T(8,128)(2,1)S(1)}, bf16[1,32,1152]{2,1,0:T(8,128)(2,1)S(1)}, u32[]{:S(2)}, u32[]{:S(2)}) collective-permute-start(bf16[1,32,1152]{2,1,0:T(8,128)(2,1)S(1)} %slice.18), channel_id=1, source_target_pairs={{0,32},{32,64},{64,96},{96,128},{128,160},{160,192},{192,224},{224... | collective-permute-start | bytes 221192 | tf_op jit(solution)/shard_map/ppermute | solution.py:15
  11.0 4.0 %copy-start.1 = (bf16[16,32,1152]{2,1,0:T(8,128)(2,1)}, bf16[16,32,1152]{2,1,0:T(8,128)(2,1)S(1)}, u32[]{:S(2)}) copy-start(bf16[16,32,1152]{2,1,0:T(8,128)(2,1)S(1)} %get-tuple-element.36) | copy-start | bytes 3538948
  12.2 1.0 copy-start.5
  17.4 13.5 %copy-start.6 = (bf16[512,1152]{1,0:T(8,128)(2,1)S(1)}, bf16[512,1152]{1,0:T(8,128)(2,1)}, u32[]{:S(2)}) copy-start(bf16[512,1152]{1,0:T(8,128)(2,1)} %copy-done.5) | copy-start | bytes 3538948
  18.6 42.5 %all-to-all-start = ((bf16[32,4,32,72]{3,2,1,0:T(8,128)(2,1)}), bf16[32,4,32,72]{3,2,1,0:T(8,128)(2,1)S(1)}, u32[]{:S(2)}, u32[]{:S(2)}) async-start(bf16[32,4,32,72]{3,2,1,0:T(8,128)(2,1)} %bitcast.8), calls=%async_computation | async-start | bytes 2097152 | tf_op jit(solution)/shard_map/all_to_all | solution.py:91
  38.4 1.5 copy-start.7
  45.5 1.2 copy-start.4
  61.1 1.0 copy-start.3
  62.1 56.4 %all-to-all-start.1 = ((bf16[32,4,32,144]{3,2,1,0:T(8,128)(2,1)}), bf16[32,4,32,144]{3,2,1,0:T(8,128)(2,1)S(1)}, u32[]{:S(2)}, u32[]{:S(2)}) async-start(bf16[32,4,32,144]{3,2,1,0:T(8,128)(2,1)} %pad_maximum_fusion), calls=%async_computation.1 | async-start | bytes 4194304 | tf_op jit(solution)/shard_map/all_to_all | solution.py:92
  118.5 1.4 copy-start.2
where the time goes:
time: 178 us; the launch traced here: 177 us
  waiting for transfers between devices  61.8 us (35%)
  blocking collectives  34.2 us (19%)
  local copies, waits for them, and re-layouts  29.8 us (17%)
  matrix products  20.7 us (12%)
  starting transfers between devices  20.2 us (11%)
  other arithmetic  8.91 us (5%)
    all_to_all x1, waiting for transfers between devices, shards(): lax.all_to_all(pair, 'tok', split_axis=0, concat_axis=2, tiled=True)  49.6 us
    all_to_all x1, blocking collectives, shards(): lax.all_to_all(att_items, 'tok', split_axis=2, concat_axis=0, tiled=True)  34.2 us
    all_to_all x1, starting transfers between devices, shards(): lax.all_to_all(to_items(query_proj), 'tok', split_axis=0, concat_axis=2,...  12.3 us
    all_to_all x1, waiting for transfers between devices, shards(): lax.all_to_all(to_items(query_proj), 'tok', split_axis=0, concat_axis=2,...  12.1 us
    dot_general x3, matrix products, project(): jnp.dot(normed, weight, preferred_element_type=jnp.float32)  7.19 us
    dot_general x4, matrix products, attend_single(): jnp.dot(attn_weights, value_rows, preferred_element_type=jnp.float32)  6.82 us
    dot_general x4, matrix products, attend_single(): jnp.dot(query_rows, key_rows.T, preferred_element_type=jnp.float32)  6.7 us
    reshape x3, local copies, waits for them, and re-layouts, to_items(): source.reshape(frames, tokens_dev, HEADS, HD).transpose(0, 2, 1, 3)  5.41 us
  transfers between devices with their start and end apart: 3, of which 2 were waited for; matrix products, arithmetic and copies ran while one was open for 13% of the time, Pallas kernels for 0%

commit v1 on v0

v1 whole, which is shorter than its diff:
```python
import functools
import math

import jax
import jax.numpy as jnp
from jax import lax
from jax.experimental import pallas as pl
from jax.experimental.pallas import tpu as pltpu
from jax.sharding import PartitionSpec as P

HEADS = 8
HD = 72
LANE = 128
SCALE_LOG2 = math.log2(math.e) / math.sqrt(HD)


def from_behind(block, axis, distance):
    devices = range(lax.axis_size(axis))
    route = [(i - distance, i) for i in devices if i - distance in devices]
    return lax.ppermute(block, axis, route)


def modulation(levels, timesteps, mod_table):
    level_count = timesteps.shape[0]
    one_hot = (levels[:, None] == jnp.arange(level_count, dtype=jnp.int32)[None, :]).astype(
        jnp.int32
    )
    noise_time = jnp.sum(one_hot * timesteps[None, :], axis=1).astype(jnp.float32)
    feature_count = mod_table.shape[1]
    frequency = jnp.exp(
        -math.log(10000.0) * jnp.arange(feature_count, dtype=jnp.float32) / feature_count
    )
    phases = noise_time[:, None] * frequency[None, :]
    offset = mod_table[0][None, :] + jnp.cos(phases)
    stretch = mod_table[1][None, :] + jnp.sin(phases)
    return (offset, stretch)


def normalize(queued, offset, stretch):
    values_f = queued.astype(jnp.float32)
    average = jnp.mean(values_f, axis=-1, keepdims=True)
    centred = values_f - average
    spread = jnp.mean(centred * centred, axis=-1, keepdims=True)
    normed = centred * lax.rsqrt(spread + 1e-06)
    return (normed * (1.0 + stretch[:, None, :]) + offset[:, None, :]).astype(jnp.bfloat16)


def pad_heads(weight):
    per_head = weight.reshape(weight.shape[0], HEADS, HD)
    return jnp.pad(per_head, ((0, 0), (0, 0), (0, LANE - HD))).reshape(weight.shape[0], -1)


def project(normed, weight):
    return jnp.dot(normed, weight, preferred_element_type=jnp.float32)


def attention_kernel(query_ref, own_ref, other_ref, out_ref):
    dims = (((1,), (1,)), ((), ()))
    width = HEADS * LANE
    for head in range(HEADS):
        cols = pl.ds(head * LANE, LANE)
        value_cols = pl.ds(width + head * LANE, LANE)
        query = query_ref[:, cols]
        score_a = lax.dot_general(
            query, own_ref[:, cols], dims, preferred_element_type=jnp.float32
        )
        score_b = lax.dot_general(
            query, other_ref[:, cols], dims, preferred_element_type=jnp.float32
        )
        peak = jnp.maximum(
            jnp.max(score_a, axis=1, keepdims=True), jnp.max(score_b, axis=1, keepdims=True)
        )
        weight_a = jnp.exp2((score_a - peak) * SCALE_LOG2).astype(jnp.bfloat16)
        weight_b = jnp.exp2((score_b - peak) * SCALE_LOG2).astype(jnp.bfloat16)
        total = jnp.dot(weight_a, own_ref[:, value_cols], preferred_element_type=jnp.float32)
        total += jnp.dot(weight_b, other_ref[:, value_cols], preferred_element_type=jnp.float32)
        out_ref[:, pl.ds(head * HD, HD)] = (total[:, :HD] / total[:, HD : HD + 1]).astype(
            out_ref.dtype
        )


def attend(query, own, other):
    rows = query.shape[0]
    vmem = pl.BlockSpec(memory_space=pltpu.VMEM)
    return pl.pallas_call(
        attention_kernel,
        out_shape=jax.ShapeDtypeStruct((rows, HEADS * HD), jnp.bfloat16),
        in_specs=[vmem] * 3,
        out_specs=vmem,
        compiler_params=pltpu.CompilerParams(vmem_limit_bytes=48 * 2**20),
        name="attention",
    )(query, own, other)


def shards(latents, new_frame, levels, timesteps, mod_table, w_query, w_key, w_value):
    frames, tokens_dev, model_width = latents.shape
    groups = lax.axis_size("tok")
    incoming = from_behind(latents[-1:], "band", 1)
    head_frame = jnp.where(lax.axis_index("band") == 0, new_frame[None], incoming)
    queued = jnp.concatenate([head_frame, latents[:-1]], axis=0)
    offset, stretch = modulation(levels, timesteps, mod_table)
    normed = normalize(queued, offset, stretch)
    sent = normed.reshape(groups, frames * tokens_dev // groups, model_width)
    mine = lax.all_to_all(sent, "tok", split_axis=0, concat_axis=0, tiled=True)
    mine = mine.reshape(frames * tokens_dev, model_width)
    w_pair = jnp.concatenate([pad_heads(w_key), pad_heads(w_value)], axis=1)
    lane = jnp.arange(2 * HEADS * LANE)
    ones = ((lane >= HEADS * LANE) & (lane % LANE == HD)).astype(jnp.float32)
    own = (project(mine, w_pair) + ones[None, :]).astype(jnp.bfloat16)
    other = lax.ppermute(own, "tok", [(i, i ^ 1) for i in range(groups)])
    query = project(mine, pad_heads(w_query)).astype(jnp.bfloat16)
    result = attend(query, own, other)
    back = lax.all_to_all(
        result.reshape(groups, -1, HEADS * HD), "tok", split_axis=0, concat_axis=0, tiled=True
    )
    return (queued, back.reshape(frames, tokens_dev, HEADS * HD))


def solution(mesh):
    in_specs = (P("band", "tok", None), P("tok", None), P("band"), P(), P(), P(), P(), P())
    out_specs = (P("band", "tok", None), P("band", "tok", None))
    return jax.shard_map(shards, mesh=mesh, in_specs=in_specs, out_specs=out_specs, check_vma=False)
```

time: 178 us -> 99.6 us (0.56)
  the two profiles are of different devices: /device:TPU:56 before, /device:TPU:97 now
where the time goes in v1:
time: 99.6 us; the launch traced here: 99.2 us
  waiting for transfers between devices  32.4 us (33%)
  blocking collectives  25.1 us (25%)
  starting transfers between devices  18.6 us (19%)
  local copies, waits for them, and re-layouts  6.83 us (7%)
  matrix products  6.22 us (6%)
  Pallas kernels  5.71 us (6%)
  other arithmetic  3.57 us (4%)
    all_to_all x1, waiting for transfers between devices, shards(): mine = lax.all_to_all(sent, 'tok', split_axis=0, concat_axis=0, tiled=True)  29.1 us
    all_to_all x1, blocking collectives, shards(): lax.all_to_all(result.reshape(groups, -1, HEADS * HD), 'tok', split_axis=...  25.1 us
    all_to_all x1, starting transfers between devices, shards(): mine = lax.all_to_all(sent, 'tok', split_axis=0, concat_axis=0, tiled=True)  13.8 us
    dot_general x2, matrix products, project(): return jnp.dot(normed, weight, preferred_element_type=jnp.float32)  6.22 us
    pallas_call x1, Pallas kernels, attend(): pl.pallas_call(attention_kernel, out_shape=jax.ShapeDtypeStruct((rows, HE...  5.71 us
    pad x3, local copies, waits for them, and re-layouts, pad_heads(): jnp.pad(per_head, ((0, 0), (0, 0), (0, LANE - HD)))  3.71 us
    ppermute x1, starting transfers between devices, shards(): other = lax.ppermute(own, 'tok', [(i, i ^ 1) for i in range(groups)])  2.48 us
    ppermute x1, starting transfers between devices, from_behind(): return lax.ppermute(block, axis, route)  2.29 us
  transfers between devices with their start and end apart: 3, of which 3 were waited for; matrix products, arithmetic and copies ran while one was open for 8% of the time, Pallas kernels for 0%

profile of v1, /device:TPU:97, one launch (start us, length us, event | category | flops | bytes accessed | tf_op | source)
XLA Modules:
  0.0 99.2 jit_solution(755011267335334081)
XLA Ops:
  0.6 1.0 %slice.12 = bf16[1,32,1152]{2,1,0:T(8,128)(2,1)S(1)} slice(bf16[16,32,1152]{2,1,0:T(8,128)(2,1)} %param.8), slice={[15:16], [0:32], [0:1152]} | slice | bytes 147456 | tf_op jit(solution)/shard_map/slice | solution.py:98
  1.7 2.3 %collective-permute-start = (bf16[1,32,1152]{2,1,0:T(8,128)(2,1)S(1)}, bf16[1,32,1152]{2,1,0:T(8,128)(2,1)S(1)}, u32[]{:S(2)}, u32[]{:S(2)}) collective-permute-start(bf16[1,32,1152]{2,1,0:T(8,128)(2,1)S(1)} %slice.12), channel_id=1, source_target_pairs={{0,32},{32,64},{64,96},{96,128},{128,160},{160,192},{192,224},{224... | collective-permute-start | bytes 221192 | tf_op jit(solution)/shard_map/ppermute | solution.py:20
  4.0 0.8 slice_reduce_fusion.1
  4.8 0.9 select_reduce_fusion
  5.7 0.3 fusion.7
  6.1 0.1 add.99
  6.2 0.1 mul.65
  6.4 1.6 %collective-permute-done = bf16[1,32,1152]{2,1,0:T(8,128)(2,1)S(1)} collective-permute-done((bf16[1,32,1152]{2,1,0:T(8,128)(2,1)S(1)}, bf16[1,32,1152]{2,1,0:T(8,128)(2,1)S(1)}, u32[]{:S(2)}, u32[]{:S(2)}) %collective-permute-start) | collective-permute-done | bytes 73760 | tf_op jit(solution)/shard_map/ppermute | solution.py:20
  8.0 0.2 convert_reduce_fusion
  8.3 0.5 multiply_reduce_fusion
  8.8 0.1 rsqrt.12
  8.9 1.6 %add_convert_fusion.1 = bf16[32,16,1152]{2,1,0:T(8,128)(2,1)} fusion(f32[32,1152]{1,0:T(8,128)S(1)} %add.99, f32[32,1152]{1,0:T(8,128)S(1)} %mul.65, f32[32,16]{1,0:T(8,128)S(1)} %rsqrt.12, f32[32,16]{1,0:T(8,128)S(1)} %div.15, bf16[32,16,1152]{2,1,0:T(8,128)(2,1)S(1)} %bitcast.17), kind=kLoop, calls=%fused_computation.5 | loop fusion | flops 3538944 | bytes 2658304 | tf_op jit(solution)/shard_map/convert_element_type | solution.py:45
  10.5 13.8 %all-to-all-start = ((bf16[32,16,1152]{2,1,0:T(8,128)(2,1)}), bf16[32,16,1152]{2,1,0:T(8,128)(2,1)S(1)}, u32[]{:S(2)}, u32[]{:S(2)}) async-start(bf16[32,16,1152]{2,1,0:T(8,128)(2,1)} %add_convert_fusion.1), calls=%async_computation | async-start | bytes 2359296 | tf_op jit(solution)/shard_map/all_to_all | solution.py:104
  24.3 1.7 %pad.11 = bf16[1152,8,128]{0,2,1:T(8,128)(2,1)S(1)} pad(bf16[1152,8,72]{0,2,1:T(8,128)(2,1)} %bitcast.22, bf16[]{:T(256)} %constant.40.clone.1), padding=0_0x0_0x0_56 | pad | bytes 3686402 | tf_op jit(solution)/shard_map/jit(_pad)/pad | solution.py:50
  26.1 1.7 %pad.12 = bf16[1152,8,128]{0,2,1:T(8,128)(2,1)} pad(bf16[1152,8,72]{0,2,1:T(8,128)(2,1)S(1)} %bitcast.23, bf16[]{:T(256)} %constant.40.clone.1), padding=0_0x0_0x0_56 | pad | bytes 3686402 | tf_op jit(solution)/shard_map/jit(_pad)/pad | solution.py:50
  27.8 29.1 %all-to-all-done = bf16[32,16,1152]{2,1,0:T(8,128)(2,1)S(1)} async-done(((bf16[32,16,1152]{2,1,0:T(8,128)(2,1)}), bf16[32,16,1152]{2,1,0:T(8,128)(2,1)S(1)}, u32[]{:S(2)}, u32[]{:S(2)}) %all-to-all-start) | async-done | bytes 1179680 | tf_op jit(solution)/shard_map/all_to_all | solution.py:104
  56.9 4.7 %add_convert_fusion.own_ref = bf16[512,2048]{1,0:T(8,128)(2,1)S(1)} fusion(bf16[512,1152]{1,0:T(8,128)(2,1)S(1)} %bitcast.25, bf16[1152,1024]{0,1:T(8,128)(2,1)} %bitcast.20, bf16[1152,1024]{0,1:T(8,128)(2,1)S(1)} %bitcast.19, f32[2048]{0:T(1024)S(1)} %fusion.13), kind=kOutput, calls=%fused_computation.4 | convolution fusion | flops 2427453440 | bytes 8003584 | tf_op jit(solution)/shard_map/dot_general | solution.py:54
  61.5 2.5 %collective-permute-start.1 = (bf16[512,2048]{1,0:T(8,128)(2,1)S(1)}, bf16[512,2048]{1,0:T(8,128)(2,1)S(1)}, u32[]{:S(2)}, u32[]{:S(2)}) collective-permute-start(bf16[512,2048]{1,0:T(8,128)(2,1)S(1)} %add_convert_fusion.own_ref), channel_id=1, source_target_pairs={{0,1},{1,0},{2,3},{3,2},{4,5},{5,4},{6,7},{7,6},{8,9},{9,8},{10,11... | collective-permute-start | bytes 6291464 | tf_op jit(solution)/shard_map/ppermute | solution.py:110
  64.0 0.3 pad.10
  64.3 1.5 %convolution_convert_fusion.query_ref = bf16[512,1024]{1,0:T(8,128)(2,1)S(1)} fusion(bf16[512,1152]{1,0:T(8,128)(2,1)S(1)} %bitcast.26, bf16[1152,1024]{0,1:T(8,128)(2,1)S(1)} %bitcast.21), kind=kOutput, calls=%fused_computation.7 | convolution fusion | flops 1208483840 | bytes 4587520 | tf_op jit(solution)/shard_map/dot_general | solution.py:54
  65.9 1.7 %collective-permute-done.1.other_ref = bf16[512,2048]{1,0:T(8,128)(2,1)S(1)} collective-permute-done((bf16[512,2048]{1,0:T(8,128)(2,1)S(1)}, bf16[512,2048]{1,0:T(8,128)(2,1)S(1)}, u32[]{:S(2)}, u32[]{:S(2)}) %collective-permute-start.1) | collective-permute-done | bytes 2097184 | tf_op jit(solution)/shard_map/ppermute | solution.py:110
  67.6 5.7 %attention.1 = bf16[512,576]{1,0:T(8,128)(2,1)S(1)} custom-call(bf16[512,1024]{1,0:T(8,128)(2,1)S(1)} %convolution_convert_fusion.query_ref, bf16[512,2048]{1,0:T(8,128)(2,1)S(1)} %add_convert_fusion.own_ref, bf16[512,2048]{1,0:T(8,128)(2,1)S(1)} %collective-permute-done.1.other_ref), custom_call_target="tpu_custom_call" | custom-call | tf_op jit(solution)/shard_map/attention/pallas_call | solution.py:85
  73.3 25.1 %all_to_all.10 = bf16[32,16,576]{2,1,0:T(8,128)(2,1)S(1)} all-to-all(bf16[32,16,576]{2,1,0:T(8,128)(2,1)S(1)} %bitcast.16), channel_id=1, replica_groups=mesh['band'=16,'tok'=32] {'tok'}, dimensions={0} | all-to-all | bytes 1179648 | tf_op jit(solution)/shard_map/all_to_all | solution.py:113
  98.4 0.8 copy.11
  (19 shorter events, 0.3 us)
Async XLA Ops:
  0.6 7.3 %slice-start = ((bf16[16,32,1152]{2,1,0:T(8,128)(2,1)}), bf16[15,32,1152]{2,1,0:T(8,128)(2,1)S(1)}, s32[]{:S(2)}) async-start(bf16[16,32,1152]{2,1,0:T(8,128)(2,1)} %param.8), calls=%async_computation.2 | async-start | bytes 2211840 | tf_op jit(solution)/shard_map/slice | solution.py:100
  0.6 7.3 %copy-start.3 = (bf16[32,1152]{1,0:T(8,128)(2,1)S(1)}, bf16[32,1152]{1,0:T(8,128)(2,1)}, u32[]{:S(2)}) copy-start(bf16[32,1152]{1,0:T(8,128)(2,1)} %param.9) | copy-start | bytes 221188
  1.7 6.3 %collective-permute-start = (bf16[1,32,1152]{2,1,0:T(8,128)(2,1)S(1)}, bf16[1,32,1152]{2,1,0:T(8,128)(2,1)S(1)}, u32[]{:S(2)}, u32[]{:S(2)}) collective-permute-start(bf16[1,32,1152]{2,1,0:T(8,128)(2,1)S(1)} %slice.12), channel_id=1, source_target_pairs={{0,32},{32,64},{64,96},{96,128},{128,160},{160,192},{192,224},{224... | collective-permute-start | bytes 221192 | tf_op jit(solution)/shard_map/ppermute | solution.py:20
  8.2 2.3 %copy-start = (bf16[16,32,1152]{2,1,0:T(8,128)(2,1)}, bf16[16,32,1152]{2,1,0:T(8,128)(2,1)S(1)}, u32[]{:S(2)}) copy-start(bf16[16,32,1152]{2,1,0:T(8,128)(2,1)S(1)} %get-tuple-element.10) | copy-start | bytes 3538948
  10.5 46.4 %all-to-all-start = ((bf16[32,16,1152]{2,1,0:T(8,128)(2,1)}), bf16[32,16,1152]{2,1,0:T(8,128)(2,1)S(1)}, u32[]{:S(2)}, u32[]{:S(2)}) async-start(bf16[32,16,1152]{2,1,0:T(8,128)(2,1)} %add_convert_fusion.1), calls=%async_computation | async-start | bytes 2359296 | tf_op jit(solution)/shard_map/all_to_all | solution.py:104
  24.3 1.7 %copy-start.1 = (bf16[1152,576]{0,1:T(8,128)(2,1)S(1)}, bf16[1152,576]{0,1:T(8,128)(2,1)}, u32[]{:S(2)}) copy-start(bf16[1152,576]{0,1:T(8,128)(2,1)} %param.15) | copy-start | bytes 3981316
  56.9 7.2 %copy-start.2 = (bf16[1152,576]{0,1:T(8,128)(2,1)S(1)}, bf16[1152,576]{0,1:T(8,128)(2,1)}, u32[]{:S(2)}) copy-start(bf16[1152,576]{0,1:T(8,128)(2,1)} %param.13) | copy-start | bytes 3981316
  61.5 6.1 %collective-permute-start.1 = (bf16[512,2048]{1,0:T(8,128)(2,1)S(1)}, bf16[512,2048]{1,0:T(8,128)(2,1)S(1)}, u32[]{:S(2)}, u32[]{:S(2)}) collective-permute-start(bf16[512,2048]{1,0:T(8,128)(2,1)S(1)} %add_convert_fusion.own_ref), channel_id=1, source_target_pairs={{0,1},{1,0},{2,3},{3,2},{4,5},{5,4},{6,7},{7,6},{8,9},{9,8},{10,11... | collective-permute-start | bytes 6291464 | tf_op jit(solution)/shard_map/ppermute | solution.py:110

commit v2 on v1

v2 whole, which is shorter than its diff:
```python
import functools
import math

import jax
import jax.numpy as jnp
from jax import lax
from jax.experimental import pallas as pl
from jax.experimental.pallas import tpu as pltpu
from jax.sharding import PartitionSpec as P

HEADS = 8
HD = 72
LANE = 128
WIDTH = 640
SCALE_LOG2 = math.log2(math.e) / math.sqrt(HD)


def from_behind(block, axis, distance):
    devices = range(lax.axis_size(axis))
    route = [(i - distance, i) for i in devices if i - distance in devices]
    return lax.ppermute(block, axis, route)


def modulation(levels, timesteps, mod_table):
    level_count = timesteps.shape[0]
    one_hot = (levels[:, None] == jnp.arange(level_count, dtype=jnp.int32)[None, :]).astype(
        jnp.int32
    )
    noise_time = jnp.sum(one_hot * timesteps[None, :], axis=1).astype(jnp.float32)
    feature_count = mod_table.shape[1]
    frequency = jnp.exp(
        -math.log(10000.0) * jnp.arange(feature_count, dtype=jnp.float32) / feature_count
    )
    phases = noise_time[:, None] * frequency[None, :]
    offset = mod_table[0][None, :] + jnp.cos(phases)
    stretch = mod_table[1][None, :] + jnp.sin(phases)
    return (offset, stretch)


def project_kernel(tokens_ref, stretch_ref, offset_ref, weight_ref, query_ref, pair_ref):
    rows = tokens_ref.shape[0]
    step = 128
    parts = []
    for start in range(0, rows, step):
        values = tokens_ref[pl.ds(start, step), :].astype(jnp.float32)
        average = jnp.mean(values, axis=-1, keepdims=True)
        centred = values - average
        spread = jnp.mean(centred * centred, axis=-1, keepdims=True)
        normed = centred * lax.rsqrt(spread + 1e-06)
        parts.append(
            (normed * (1.0 + stretch_ref[...]) + offset_ref[...]).astype(jnp.bfloat16)
        )
    normed = jnp.concatenate(parts, axis=0)
    pair_cols = pair_ref.shape[1]
    pair_ref[...] = jnp.dot(
        normed, weight_ref[:, :pair_cols], preferred_element_type=jnp.float32
    ).astype(jnp.bfloat16)
    query_ref[...] = jnp.dot(
        normed, weight_ref[:, pair_cols:], preferred_element_type=jnp.float32
    ).astype(jnp.bfloat16)


def normalize_and_project(tokens, stretch, offset, weight):
    vmem = pl.BlockSpec(memory_space=pltpu.VMEM)
    rows = tokens.shape[0]
    return pl.pallas_call(
        project_kernel,
        out_shape=(
            jax.ShapeDtypeStruct((rows, WIDTH), jnp.bfloat16),
            jax.ShapeDtypeStruct((rows, 2 * WIDTH), jnp.bfloat16),
        ),
        in_specs=[vmem] * 4,
        out_specs=(vmem, vmem),
        compiler_params=pltpu.CompilerParams(vmem_limit_bytes=24 * 2**20),
        name="project",
    )(tokens, stretch, offset, weight)


def attention_kernel(query_ref, pair_ref, out_ref):
    dims = (((1,), (1,)), ((), ()))
    window = 2 * LANE
    rows, keys = query_ref.shape[0], pair_ref.shape[0]
    lane_q = lax.broadcasted_iota(jnp.int32, (rows, window), 1)
    lane_k = lax.broadcasted_iota(jnp.int32, (keys, window), 1)
    done = None
    for head in range(HEADS):
        start = head * HD // LANE * LANE
        first = head * HD - start
        query = query_ref[:, pl.ds(start, window)]
        key = pair_ref[:, pl.ds(start, window)]
        value = pair_ref[:, pl.ds(WIDTH + start, window)]
        query = jnp.where((lane_q >= first) & (lane_q < first + HD), query, 0)
        value = jnp.where((lane_k >= first) & (lane_k < first + HD), value, 1)
        score = lax.dot_general(query, key, dims, preferred_element_type=jnp.float32)
        peak = jnp.max(score, axis=1, keepdims=True)
        weight = jnp.exp2((score - peak) * SCALE_LOG2).astype(jnp.bfloat16)
        total = jnp.dot(weight, value, preferred_element_type=jnp.float32)
        at = first + HD if first + HD < window else 0
        result = total / total[:, at : at + 1]
        if done is None:
            done = result
        else:
            if start != done_start:
                out_ref[:, pl.ds(done_start, LANE)] = done[:, :LANE].astype(out_ref.dtype)
                done = jnp.concatenate([done[:, LANE:], result[:, LANE:]], axis=1)
            done = jnp.where(lane_q < first, done, result)
        done_start = start
    tail = HEADS * HD - done_start
    out_ref[:, pl.ds(done_start, tail)] = done[:, :tail].astype(out_ref.dtype)


def attend(query, pair):
    vmem = pl.BlockSpec(memory_space=pltpu.VMEM)
    return pl.pallas_call(
        attention_kernel,
        out_shape=jax.ShapeDtypeStruct((query.shape[0], HEADS * HD), jnp.bfloat16),
        in_specs=[vmem] * 2,
        out_specs=vmem,
        compiler_params=pltpu.CompilerParams(vmem_limit_bytes=32 * 2**20),
        name="attention",
    )(query, pair)


def shards(latents, new_frame, levels, timesteps, mod_table, w_query, w_key, w_value):
    frames, tokens_dev, model_width = latents.shape
    groups = lax.axis_size("tok")
    cores = groups // frames
    same_core = [[cores * i + core for i in range(frames)] for core in range(cores)]
    same_chip = [[cores * i + core for core in range(cores)] for i in range(frames)]
    incoming = from_behind(latents[-1:], "band", 1)
    head_frame = jnp.where(lax.axis_index("band") == 0, new_frame[None], incoming)
    queued = jnp.concatenate([head_frame, latents[:-1]], axis=0)
    mine = lax.all_to_all(
        queued, "tok", split_axis=0, concat_axis=0, axis_index_groups=same_core, tiled=True
    )
    mine = mine.reshape(frames * tokens_dev, model_width)
    level = lax.dynamic_slice_in_dim(levels, lax.axis_index("tok") // cores, 1)
    offset, stretch = modulation(level, timesteps, mod_table)
    gap = jnp.zeros((model_width, WIDTH - HEADS * HD), w_key.dtype)
    weights = jnp.concatenate([w_key, gap, w_value, gap, w_query, gap], axis=1)
    query, own = normalize_and_project(mine, stretch, offset, weights)
    pair = lax.all_gather(own, "tok", axis=0, axis_index_groups=same_chip, tiled=True)
    result = attend(query, pair)
    back = lax.all_to_all(
        result.reshape(frames, tokens_dev, HEADS * HD),
        "tok",
        split_axis=0,
        concat_axis=0,
        axis_index_groups=same_core,
        tiled=True,
    )
    return (queued, back)


def solution(mesh):
    in_specs = (P("band", "tok", None), P("tok", None), P("band"), P(), P(), P(), P(), P())
    out_specs = (P("band", "tok", None), P("band", "tok", None))
    return jax.shard_map(shards, mesh=mesh, in_specs=in_specs, out_specs=out_specs, check_vma=False)
```

time: 99.6 us -> 130 us (1.31)
  the two profiles are of different devices: /device:TPU:97 before, /device:TPU:56 now
where the time goes in v2:
time: 130 us; the launch traced here: 129 us
  waiting for transfers between devices  32.2 us (25%)
  blocking collectives  31.8 us (24%)
  local copies, waits for them, and re-layouts  21.5 us (17%)
  starting transfers between devices  16.5 us (13%)
  between operations  14.7 us (11%)
  Pallas kernels  9.51 us (7%)
  other arithmetic  2.59 us (2%)
    all_to_all x1, blocking collectives, shards(): lax.all_to_all(result.reshape(frames, tokens_dev, HEADS * HD), 'tok', spl...  31.8 us
    all_gather x1, waiting for transfers between devices, shards(): lax.all_gather(own, 'tok', axis=0, axis_index_groups=same_chip, tiled=True)  21.1 us
    all_to_all x1, starting transfers between devices, shards(): lax.all_to_all(queued, 'tok', split_axis=0, concat_axis=0, axis_index_gro...  13 us
    unnamed x16, local copies, waits for them, and re-layouts  12.2 us
    all_to_all x1, waiting for transfers between devices, shards(): lax.all_to_all(queued, 'tok', split_axis=0, concat_axis=0, axis_index_gro...  8.31 us
    concatenate x1, local copies, waits for them, and re-layouts, shards(): weights = jnp.concatenate([w_key, gap, w_value, gap, w_query, gap], axis=1)  7.73 us
    pallas_call x1, Pallas kernels, attend(): pl.pallas_call(attention_kernel, out_shape=jax.ShapeDtypeStruct((query.sh...  5.71 us
    pallas_call x1, Pallas kernels, normalize_and_project(): pl.pallas_call(project_kernel, out_shape=(jax.ShapeDtypeStruct((rows, WID...  3.81 us
  transfers between devices with their start and end apart: 3, of which 3 were waited for; matrix products, arithmetic and copies ran while one was open for 13% of the time, Pallas kernels for 0%

profile of v2, /device:TPU:56, one launch (start us, length us, event | category | flops | bytes accessed | tf_op | source)
XLA Modules:
  0.0 128.9 jit_solution(5780631273327976083)
XLA Ops:
  7.2 0.0 slice-start
  7.2 1.0 slice.12
  8.2 3.5 %collective-permute-start = (bf16[1,32,1152]{2,1,0:T(8,128)(2,1)S(1)}, bf16[1,32,1152]{2,1,0:T(8,128)(2,1)S(1)}, u32[]{:S(2)}, u32[]{:S(2)}) collective-permute-start(bf16[1,32,1152]{2,1,0:T(8,128)(2,1)S(1)} %slice.12), channel_id=1, source_target_pairs={{0,32},{32,64},{64,96},{96,128},{128,160},{160,192},{192,224},{224... | collective-permute-start | bytes 221192 | tf_op jit(solution)/shard_map/ppermute | solution.py:21
  11.7 2.7 %collective-permute-done = bf16[1,32,1152]{2,1,0:T(8,128)(2,1)S(1)} collective-permute-done((bf16[1,32,1152]{2,1,0:T(8,128)(2,1)S(1)}, bf16[1,32,1152]{2,1,0:T(8,128)(2,1)S(1)}, u32[]{:S(2)}, u32[]{:S(2)}) %collective-permute-start) | collective-permute-done | bytes 73760 | tf_op jit(solution)/shard_map/ppermute | solution.py:21
  14.5 1.1 pad_maximum_fusion
  15.6 13.0 %all-to-all-start = ((bf16[16,32,1152]{2,1,0:T(8,128)(2,1)}), bf16[16,32,1152]{2,1,0:T(8,128)(2,1)S(1)}, u32[]{:S(2)}, u32[]{:S(2)}) async-start(bf16[16,32,1152]{2,1,0:T(8,128)(2,1)} %pad_maximum_fusion), calls=%async_computation | async-start | bytes 2359296 | tf_op jit(solution)/shard_map/all_to_all | solution.py:133
  28.6 0.0 all-gather.2.cloned.1.call-start
  28.7 0.6 dynamic_slice.3
  29.3 1.3 fusion
  31.1 2.1 %copy.12 = bf16[1152,576]{1,0:T(8,128)(2,1)S(1)} copy(bf16[1152,576]{0,1:T(8,128)(2,1)} %param.13) | data formatting | bytes 2654208 | tf_op args[5]
  33.2 2.6 %copy.10 = bf16[1152,576]{1,0:T(8,128)(2,1)} copy(bf16[1152,576]{0,1:T(8,128)(2,1)} %param.14) | data formatting | bytes 2654208 | tf_op args[6]
  35.8 2.6 %copy.11 = bf16[1152,576]{1,0:T(8,128)(2,1)} copy(bf16[1152,576]{0,1:T(8,128)(2,1)} %param.15) | data formatting | bytes 2654208 | tf_op args[7]
  38.5 0.0 copy-start.3
  38.5 7.7 %concatenate.7.weight_ref = bf16[1152,1920]{1,0:T(8,128)(2,1)} concatenate(bf16[1152,576]{1,0:T(8,128)(2,1)} %copy.10, bf16[1152,64]{1,0:T(8,128)(2,1)S(1)} %broadcast_in_dim.5, bf16[1152,576]{1,0:T(8,128)(2,1)} %copy.11, bf16[1152,64]{1,0:T(8,128)(2,1)S(1)} %broadcast_in_dim.5, bf16[1152,576]{1,0:T(8,128)(2,1)S(1)} %copy.12, bf16[1152,64]{1,0:T(8,128)(2,1)S(1)} %broadcast_in_dim.5), dimensions={1} | concatenate | bytes 8847360 | tf_op jit(solution)/shard_map/concatenate | solution.py:140
  46.2 0.2 cosine_add_fusion
  46.4 8.3 %all-to-all-done = bf16[16,32,1152]{2,1,0:T(8,128)(2,1)S(1)} async-done(((bf16[16,32,1152]{2,1,0:T(8,128)(2,1)}), bf16[16,32,1152]{2,1,0:T(8,128)(2,1)S(1)}, u32[]{:S(2)}, u32[]{:S(2)}) %all-to-all-start) | async-done | bytes 1179680 | tf_op jit(solution)/shard_map/all_to_all | solution.py:133
  54.7 2.3 %copy-done = bf16[1152,1920]{1,0:T(8,128)(2,1)S(1)} copy-done((bf16[1152,1920]{1,0:T(8,128)(2,1)S(1)}, bf16[1152,1920]{1,0:T(8,128)(2,1)}, u32[]{:S(2)}) %copy-start) | copy-done | bytes 4423704
  57.0 3.8 %project.1 = (bf16[512,640]{1,0:T(8,128)(2,1)S(1)}, bf16[512,1280]{1,0:T(8,128)(2,1)}) custom-call(bf16[512,1152]{1,0:T(8,128)(2,1)S(1)} %bitcast.5, f32[1,1152]{1,0:T(1,128)S(1)} %get-tuple-element.7.stretch_ref, f32[1,1152]{1,0:T(1,128)S(1)} %get-tuple-element.6.offset_ref, bf16[1152,1920]{1,0:T(8,128)(2,1)S(1)} %copy-done), custom_call_target="tpu_custom_call" | custom-call | tf_op jit(solution)/shard_map/project/pallas_call | solution.py:66
  60.8 0.0 all-gather.2.cloned.1.call-update
  60.8 21.1 %all-gather.2.cloned.1.call-done.pair_ref = bf16[1024,1280]{1,0:T(8,128)(2,1)} async-done(((bf16[512,1280]{1,0:T(8,128)(2,1)}), bf16[1024,1280]{1,0:T(8,128)(2,1)}) %all-gather.2.cloned.1.call-update) | async-done | bytes 2621456 | tf_op jit(solution)/shard_map/all_gather | solution.py:142
  81.9 1.7 %copy-done.1 = bf16[1024,1280]{1,0:T(8,128)(2,1)S(1)} copy-done((bf16[1024,1280]{1,0:T(8,128)(2,1)S(1)}, bf16[1024,1280]{1,0:T(8,128)(2,1)}, u32[]{:S(2)}) %copy-start.1) | copy-done | bytes 2621464
  83.7 5.7 %attention.1 = bf16[512,576]{1,0:T(8,128)(2,1)S(1)} custom-call(bf16[512,640]{1,0:T(8,128)(2,1)S(1)} %get-tuple-element.4.query_ref, bf16[1024,1280]{1,0:T(8,128)(2,1)S(1)} %copy-done.1), custom_call_target="tpu_custom_call" | custom-call | tf_op jit(solution)/shard_map/attention/pallas_call | solution.py:114
  89.4 31.8 %all_to_all.10 = bf16[16,32,576]{2,1,0:T(8,128)(2,1)S(1)} all-to-all(bf16[16,32,576]{2,1,0:T(8,128)(2,1)S(1)} %bitcast.6), channel_id=1, replica_groups={{0,2,4,6,8,10,12,14,16,18,20,22,24,26,28,30},{1,3,5,7,9,11,13,15,17,19,..., dimensions={0} | all-to-all | bytes 1179648 | tf_op jit(solution)/shard_map/all_to_all | solution.py:144
  121.2 0.8 copy.14
  (12 shorter events, 0.1 us)
Async XLA Ops:
  7.2 7.3 %slice-start = ((bf16[16,32,1152]{2,1,0:T(8,128)(2,1)}), bf16[15,32,1152]{2,1,0:T(8,128)(2,1)S(1)}, s32[]{:S(2)}) async-start(bf16[16,32,1152]{2,1,0:T(8,128)(2,1)} %param.8), calls=%async_computation.3 | async-start | bytes 2211840 | tf_op jit(solution)/shard_map/slice | solution.py:132
  7.2 7.3 %copy-start.2 = (bf16[32,1152]{1,0:T(8,128)(2,1)S(1)}, bf16[32,1152]{1,0:T(8,128)(2,1)}, u32[]{:S(2)}) copy-start(bf16[32,1152]{1,0:T(8,128)(2,1)} %param.9) | copy-start | bytes 221188
  8.2 6.2 %collective-permute-start = (bf16[1,32,1152]{2,1,0:T(8,128)(2,1)S(1)}, bf16[1,32,1152]{2,1,0:T(8,128)(2,1)S(1)}, u32[]{:S(2)}, u32[]{:S(2)}) collective-permute-start(bf16[1,32,1152]{2,1,0:T(8,128)(2,1)S(1)} %slice.12), channel_id=1, source_target_pairs={{0,32},{32,64},{64,96},{96,128},{128,160},{160,192},{192,224},{224... | collective-permute-start | bytes 221192 | tf_op jit(solution)/shard_map/ppermute | solution.py:21
  15.6 13.1 %copy-start.5 = (s32[16]{0:T(128)S(1)}, s32[16]{0:T(128)}, u32[]{:S(2)}) copy-start(s32[16]{0:T(128)} %param.10) | copy-start | bytes 196
  15.6 13.7 %copy-start.4 = (s32[256]{0:T(256)S(1)}, s32[256]{0:T(256)}, u32[]{:S(2)}) copy-start(s32[256]{0:T(256)} %param.11) | copy-start | bytes 3076
  15.6 39.1 %all-to-all-start = ((bf16[16,32,1152]{2,1,0:T(8,128)(2,1)}), bf16[16,32,1152]{2,1,0:T(8,128)(2,1)S(1)}, u32[]{:S(2)}, u32[]{:S(2)}) async-start(bf16[16,32,1152]{2,1,0:T(8,128)(2,1)} %pad_maximum_fusion), calls=%async_computation | async-start | bytes 2359296 | tf_op jit(solution)/shard_map/all_to_all | solution.py:133
  28.6 53.3 %all-gather.2.cloned.1.call-start = ((), (), s32[]{:S(2)}) async-start(), calls=%async_computation.2 | async-start | bytes 3932160 | tf_op jit(solution)/shard_map/all_gather | solution.py:142
  38.5 7.7 %copy-start.3 = (f32[2,1152]{1,0:T(2,128)S(1)}, f32[2,1152]{1,0:T(2,128)}, u32[]{:S(2)}) copy-start(f32[2,1152]{1,0:T(2,128)} %param.12) | copy-start | bytes 27652
  54.7 2.3 %copy-start = (bf16[1152,1920]{1,0:T(8,128)(2,1)S(1)}, bf16[1152,1920]{1,0:T(8,128)(2,1)}, u32[]{:S(2)}) copy-start(bf16[1152,1920]{1,0:T(8,128)(2,1)} %concatenate.7.weight_ref) | copy-start | bytes 13271044
  81.9 1.7 %copy-start.1 = (bf16[1024,1280]{1,0:T(8,128)(2,1)S(1)}, bf16[1024,1280]{1,0:T(8,128)(2,1)}, u32[]{:S(2)}) copy-start(bf16[1024,1280]{1,0:T(8,128)(2,1)} %all-gather.2.cloned.1.call-done.pair_ref) | copy-start | bytes 7864324
Sparse Core Ops, SparseCore 0:
  60.9 20.9 all-gather.1

commit v3 on v2

v3 whole, which is shorter than its diff:
```python
import functools
import math

import jax
import jax.numpy as jnp
from jax import lax
from jax.experimental import pallas as pl
from jax.experimental.pallas import tpu as pltpu
from jax.sharding import PartitionSpec as P

HEADS = 8
HD = 72
LANE = 128
WIDTH = 640
SCALE_LOG2 = math.log2(math.e) / math.sqrt(HD)


def from_behind(block, axis, distance):
    devices = range(lax.axis_size(axis))
    route = [(i - distance, i) for i in devices if i - distance in devices]
    return lax.ppermute(block, axis, route)


def modulation(levels, timesteps, mod_table):
    level_count = timesteps.shape[0]
    one_hot = (levels[:, None] == jnp.arange(level_count, dtype=jnp.int32)[None, :]).astype(
        jnp.int32
    )
    noise_time = jnp.sum(one_hot * timesteps[None, :], axis=1).astype(jnp.float32)
    feature_count = mod_table.shape[1]
    frequency = jnp.exp(
        -math.log(10000.0) * jnp.arange(feature_count, dtype=jnp.float32) / feature_count
    )
    phases = noise_time[:, None] * frequency[None, :]
    offset = mod_table[0][None, :] + jnp.cos(phases)
    stretch = mod_table[1][None, :] + jnp.sin(phases)
    return (offset, stretch)


def project_kernel(
    tokens_ref, stretch_ref, offset_ref, weight_hbm, normed_ref, pair_ref, weight_ref, arrived
):
    rows, depth = tokens_ref.shape
    pieces = arrived.shape[0]
    piece = depth // pieces
    copies = [
        pltpu.make_async_copy(
            weight_hbm.at[pl.ds(i * piece, piece)],
            weight_ref.at[pl.ds(i * piece, piece)],
            arrived.at[i],
        )
        for i in range(pieces)
    ]
    for copy in copies:
        copy.start()
    half, step = rows // 2, 64

    def normalized(first):
        parts = []
        for start in range(first, first + half, step):
            values = tokens_ref[pl.ds(start, step), :].astype(jnp.float32)
            average = jnp.mean(values, axis=-1, keepdims=True)
            centred = values - average
            spread = jnp.mean(centred * centred, axis=-1, keepdims=True)
            normed = centred * lax.rsqrt(spread + 1e-06)
            parts.append(
                (normed * (1.0 + stretch_ref[...]) + offset_ref[...]).astype(jnp.bfloat16)
            )
        normed = jnp.concatenate(parts, axis=0)
        normed_ref[pl.ds(first, half), :] = normed
        return normed

    def project(normed, first):
        pair_ref[pl.ds(first, half), :] = jnp.dot(
            normed, weight_ref[...], preferred_element_type=jnp.float32
        ).astype(jnp.bfloat16)

    upper = normalized(0)
    for copy in copies:
        copy.wait()
    project(upper, 0)
    project(normalized(half), half)


def normalize_and_project(tokens, stretch, offset, weight):
    vmem = pl.BlockSpec(memory_space=pltpu.VMEM)
    rows, width = tokens.shape[0], weight.shape[1]
    return pl.pallas_call(
        project_kernel,
        out_shape=(
            jax.ShapeDtypeStruct(tokens.shape, jnp.bfloat16),
            jax.ShapeDtypeStruct((rows, width), jnp.bfloat16),
        ),
        in_specs=[vmem] * 3 + [pl.BlockSpec(memory_space=pltpu.HBM)],
        out_specs=(vmem, vmem),
        scratch_shapes=[
            pltpu.VMEM(weight.shape, jnp.bfloat16),
            pltpu.SemaphoreType.DMA((4,)),
        ],
        compiler_params=pltpu.CompilerParams(vmem_limit_bytes=24 * 2**20),
        name="project",
    )(tokens, stretch, offset, weight)


def attention_kernel(query_ref, own_ref, other_ref, out_ref):
    dims = (((1,), (1,)), ((), ()))
    window = 2 * LANE
    rows = query_ref.shape[0]
    lane = lax.broadcasted_iota(jnp.int32, (rows, window), 1)
    for head in range(HEADS):
        start = head * HD // LANE * LANE
        first = head * HD - start
        inside = (lane >= first) & (lane < first + HD)
        query = jnp.where(inside, query_ref[:, pl.ds(start, window)], 0)
        scores = [
            lax.dot_general(
                query, pair[:, pl.ds(start, window)], dims, preferred_element_type=jnp.float32
            )
            for pair in (own_ref, other_ref)
        ]
        peak = jnp.maximum(*(jnp.max(score, axis=1, keepdims=True) for score in scores))
        total = 0.0
        for score, pair in zip(scores, (own_ref, other_ref)):
            weight = jnp.exp2((score - peak) * SCALE_LOG2).astype(jnp.bfloat16)
            value = jnp.where(inside, pair[:, pl.ds(WIDTH + start, window)], 1)
            total += jnp.dot(weight, value, preferred_element_type=jnp.float32)
        at = first + HD if first + HD < window else 0
        result = total / total[:, at : at + 1]
        if head == 0:
            done = result
        else:
            if start != done_start:
                out_ref[:, pl.ds(done_start, LANE)] = done[:, :LANE].astype(out_ref.dtype)
                done = jnp.concatenate([done[:, LANE:], result[:, LANE:]], axis=1)
            done = jnp.where(lane < first, done, result)
        done_start = start
    tail = HEADS * HD - done_start
    out_ref[:, pl.ds(done_start, tail)] = done[:, :tail].astype(out_ref.dtype)


def attend(query, own, other):
    vmem = pl.BlockSpec(memory_space=pltpu.VMEM)
    return pl.pallas_call(
        attention_kernel,
        out_shape=jax.ShapeDtypeStruct((query.shape[0], HEADS * HD), jnp.bfloat16),
        in_specs=[vmem] * 3,
        out_specs=vmem,
        compiler_params=pltpu.CompilerParams(vmem_limit_bytes=32 * 2**20),
        name="attention",
    )(query, own, other)


def shards(latents, new_frame, levels, timesteps, mod_table, w_query, w_key, w_value):
    frames, tokens_dev, model_width = latents.shape
    groups = lax.axis_size("tok")
    cores = groups // frames
    same_core = [[cores * i + core for i in range(frames)] for core in range(cores)]
    incoming = from_behind(latents[-1:], "band", 1)
    head_frame = jnp.where(lax.axis_index("band") == 0, new_frame[None], incoming)
    moved = lax.optimization_barrier(jnp.concatenate([new_frame[None], latents[:-1]], axis=0))
    queued = lax.dynamic_update_slice_in_dim(moved, head_frame, 0, axis=0)
    mine = lax.all_to_all(
        queued, "tok", split_axis=0, concat_axis=0, axis_index_groups=same_core, tiled=True
    )
    mine = mine.reshape(frames * tokens_dev, model_width)
    level = lax.dynamic_slice_in_dim(levels, lax.axis_index("tok") // cores, 1)
    offset, stretch = modulation(level, timesteps, mod_table)
    gap = jnp.zeros((model_width, WIDTH - HEADS * HD), w_key.dtype)
    w_pair = jnp.concatenate([w_key, gap, w_value, gap], axis=1)
    normed, own = normalize_and_project(mine, stretch, offset, w_pair)
    other = lax.ppermute(own, "tok", [(i, i ^ 1) for i in range(groups)])
    query = jnp.dot(
        normed, jnp.concatenate([w_query, gap], axis=1), preferred_element_type=jnp.float32
    ).astype(jnp.bfloat16)
    result = attend(query, own, other)
    back = lax.all_to_all(
        result.reshape(frames, tokens_dev, HEADS * HD),
        "tok",
        split_axis=0,
        concat_axis=0,
        axis_index_groups=same_core,
        tiled=True,
    )
    return (queued, back)


def solution(mesh):
    in_specs = (P("band", "tok", None), P("tok", None), P("band"), P(), P(), P(), P(), P())
    out_specs = (P("band", "tok", None), P("band", "tok", None))
    return jax.shard_map(shards, mesh=mesh, in_specs=in_specs, out_specs=out_specs, check_vma=False)
```

time: 130 us -> 94 us (0.72)
  the two profiles are of different devices: /device:TPU:56 before, /device:TPU:64 now
where the time goes in v3:
time: 94 us; the launch traced here: 93.6 us
  blocking collectives  25 us (27%)
  waiting for transfers between devices  23.6 us (25%)
  starting transfers between devices  17.5 us (19%)
  local copies, waits for them, and re-layouts  10.8 us (11%)
  Pallas kernels  10.8 us (11%)
  other arithmetic  3.26 us (3%)
  between operations  1.44 us (2%)
  matrix products  1.18 us (1%)
    all_to_all x1, blocking collectives, shards(): lax.all_to_all(result.reshape(frames, tokens_dev, HEADS * HD), 'tok', spl...  25 us
    all_to_all x1, waiting for transfers between devices, shards(): lax.all_to_all(queued, 'tok', split_axis=0, concat_axis=0, axis_index_gro...  18.1 us
    all_to_all x1, starting transfers between devices, shards(): lax.all_to_all(queued, 'tok', split_axis=0, concat_axis=0, axis_index_gro...  12.1 us
    pallas_call x1, Pallas kernels, attend(): pl.pallas_call(attention_kernel, out_shape=jax.ShapeDtypeStruct((query.sh...  5.77 us
    pallas_call x1, Pallas kernels, normalize_and_project(): pl.pallas_call(project_kernel, out_shape=(jax.ShapeDtypeStruct(tokens.sha...  5.05 us
    concatenate x1, local copies, waits for them, and re-layouts, shards(): w_pair = jnp.concatenate([w_key, gap, w_value, gap], axis=1)  4.98 us
    unnamed x17, local copies, waits for them, and re-layouts  4.16 us
    ppermute x1, waiting for transfers between devices, from_behind(): return lax.ppermute(block, axis, route)  3.71 us
  transfers between devices with their start and end apart: 3, of which 3 were waited for; matrix products, arithmetic and copies ran while one was open for 14% of the time, Pallas kernels for 0%

profile of v3, /device:TPU:64, one launch (start us, length us, event | category | flops | bytes accessed | tf_op | source)
XLA Modules:
  0.0 93.6 jit_solution(8971633073986876605)
XLA Ops:
  0.6 0.0 slice-start
  0.6 1.0 %slice.13 = bf16[1,32,1152]{2,1,0:T(8,128)(2,1)S(1)} slice(bf16[16,32,1152]{2,1,0:T(8,128)(2,1)} %param.8), slice={[15:16], [0:32], [0:1152]} | slice | bytes 147456 | tf_op jit(solution)/shard_map/slice | solution.py:158
  1.6 3.5 %collective-permute-start = (bf16[1,32,1152]{2,1,0:T(8,128)(2,1)S(1)}, bf16[1,32,1152]{2,1,0:T(8,128)(2,1)S(1)}, u32[]{:S(2)}, u32[]{:S(2)}) collective-permute-start(bf16[1,32,1152]{2,1,0:T(8,128)(2,1)S(1)} %slice.13), channel_id=1, source_target_pairs={{0,32},{32,64},{64,96},{96,128},{128,160},{160,192},{192,224},{224... | collective-permute-start | bytes 221192 | tf_op jit(solution)/shard_map/ppermute | solution.py:21
  5.1 1.1 %pad_maximum_fusion = bf16[16,32,1152]{2,1,0:T(8,128)(2,1)} fusion(bf16[15,32,1152]{2,1,0:T(8,128)(2,1)S(1)} %slice-done, bf16[1,32,1152]{2,1,0:T(8,128)(2,1)S(1)} %bitcast.7), kind=kLoop, calls=%fused_computation.3 | loop fusion | flops 589824 | bytes 2359296 | tf_op jit(solution)/shard_map/concatenate | solution.py:160
  6.3 3.7 %collective-permute-done = bf16[1,32,1152]{2,1,0:T(8,128)(2,1)S(1)} collective-permute-done((bf16[1,32,1152]{2,1,0:T(8,128)(2,1)S(1)}, bf16[1,32,1152]{2,1,0:T(8,128)(2,1)S(1)}, u32[]{:S(2)}, u32[]{:S(2)}) %collective-permute-start) | collective-permute-done | bytes 73760 | tf_op jit(solution)/shard_map/ppermute | solution.py:21
  10.0 0.7 select_dynamic-update-slice_fusion
  10.6 12.1 %all-to-all-start = ((bf16[16,32,1152]{2,1,0:T(8,128)(2,1)}), bf16[16,32,1152]{2,1,0:T(8,128)(2,1)}, u32[]{:S(2)}, u32[]{:S(2)}) async-start(bf16[16,32,1152]{2,1,0:T(8,128)(2,1)} %select_dynamic-update-slice_fusion), calls=%async_computation | async-start | bytes 2359296 | tf_op jit(solution)/shard_map/all_to_all | solution.py:162
  22.8 0.6 dynamic_slice.3
  23.4 1.3 %fusion.5 = s32[]{:T(128)} fusion(s32[256]{0:T(256)S(1)} %copy-done.4, s32[]{:T(128)} %bitcast.2), kind=kLoop, calls=%fused_computation.9 | loop fusion | flops 767 | bytes 1032 | tf_op jit(solution)/shard_map/reduce_sum | solution.py:29
  25.4 0.0 copy-start.1
  25.4 1.7 %copy.10 = bf16[1152,576]{1,0:T(8,128)(2,1)} copy(bf16[1152,576]{0,1:T(8,128)(2,1)S(1)} %copy-done) | data formatting | bytes 2654208 | tf_op args[6]
  27.0 1.6 %copy.11 = bf16[1152,576]{1,0:T(8,128)(2,1)} copy(bf16[1152,576]{0,1:T(8,128)(2,1)S(1)} %copy-done.1) | data formatting | bytes 2654208 | tf_op args[7]
  28.7 0.0 copy-start.3
  28.7 5.0 %concatenate.10.weight_hbm = bf16[1152,1280]{1,0:T(8,128)(2,1)S(1)} concatenate(bf16[1152,576]{1,0:T(8,128)(2,1)} %copy.10, bf16[1152,64]{1,0:T(8,128)(2,1)S(1)} %broadcast_in_dim.5, bf16[1152,576]{1,0:T(8,128)(2,1)} %copy.11, bf16[1152,64]{1,0:T(8,128)(2,1)S(1)} %broadcast_in_dim.5), dimensions={1} | concatenate | bytes 5898240 | tf_op jit(solution)/shard_map/concatenate | solution.py:169
  33.7 0.2 cosine_add_fusion
  33.9 18.1 %all-to-all-done = bf16[16,32,1152]{2,1,0:T(8,128)(2,1)} async-done(((bf16[16,32,1152]{2,1,0:T(8,128)(2,1)}), bf16[16,32,1152]{2,1,0:T(8,128)(2,1)}, u32[]{:S(2)}, u32[]{:S(2)}) %all-to-all-start) | async-done | bytes 1179680 | tf_op jit(solution)/shard_map/all_to_all | solution.py:162
  52.0 5.0 %project.1 = (bf16[512,1152]{1,0:T(8,128)(2,1)S(1)}, bf16[512,1280]{1,0:T(8,128)(2,1)S(1)}) custom-call(bf16[512,1152]{1,0:T(8,128)(2,1)} %bitcast.1.tokens_ref, f32[1,1152]{1,0:T(1,128)S(1)} %get-tuple-element.7.stretch_ref, f32[1,1152]{1,0:T(1,128)S(1)} %get-tuple-element.6.offset_ref, bf16[1152,1280]{1,0:T(8,128)(2,1)S(1)} %concatenate.10.weight_hbm), custom_call_target="tpu_custom_call" | custom-call | tf_op jit(solution)/shard_map/project/pallas_call | solution.py:88
  57.0 1.9 %collective-permute-start.1 = (bf16[512,1280]{1,0:T(8,128)(2,1)S(1)}, bf16[512,1280]{1,0:T(8,128)(2,1)S(1)}, u32[]{:S(2)}, u32[]{:S(2)}) collective-permute-start(bf16[512,1280]{1,0:T(8,128)(2,1)S(1)} %get-tuple-element.5.own_ref), channel_id=1, source_target_pairs={{0,1},{1,0},{2,3},{3,2},{4,5},{5,4},{6,7},{7,6},{8,9},{9,8},{10,11... | collective-permute-start | bytes 3932168 | tf_op jit(solution)/shard_map/ppermute | solution.py:171
  59.0 0.0 copy-done.5
  59.0 1.2 %fusion.2.query_ref = bf16[512,640]{1,0:T(8,128)(2,1)S(1)} fusion(bf16[512,1152]{1,0:T(8,128)(2,1)S(1)} %get-tuple-element.4, bf16[1152,576]{0,1:T(8,128)(2,1)S(1)} %copy-done.5), kind=kOutput, calls=%fused_computation.2 | convolution fusion | flops 755302400 | bytes 3162112 | tf_op jit(solution)/shard_map/dot_general | solution.py:172
  60.2 1.8 %collective-permute-done.1.other_ref = bf16[512,1280]{1,0:T(8,128)(2,1)S(1)} collective-permute-done((bf16[512,1280]{1,0:T(8,128)(2,1)S(1)}, bf16[512,1280]{1,0:T(8,128)(2,1)S(1)}, u32[]{:S(2)}, u32[]{:S(2)}) %collective-permute-start.1) | collective-permute-done | bytes 1310752 | tf_op jit(solution)/shard_map/ppermute | solution.py:171
  62.0 5.8 %attention.1 = bf16[512,576]{1,0:T(8,128)(2,1)S(1)} custom-call(bf16[512,640]{1,0:T(8,128)(2,1)S(1)} %fusion.2.query_ref, bf16[512,1280]{1,0:T(8,128)(2,1)S(1)} %get-tuple-element.5.own_ref, bf16[512,1280]{1,0:T(8,128)(2,1)S(1)} %collective-permute-done.1.other_ref), custom_call_target="tpu_custom_call" | custom-call | tf_op jit(solution)/shard_map/attention/pallas_call | solution.py:143
  67.8 25.0 %all_to_all.10 = bf16[16,32,576]{2,1,0:T(8,128)(2,1)S(1)} all-to-all(bf16[16,32,576]{2,1,0:T(8,128)(2,1)S(1)} %bitcast.6), channel_id=1, replica_groups={{0,2,4,6,8,10,12,14,16,18,20,22,24,26,28,30},{1,3,5,7,9,11,13,15,17,19,..., dimensions={0} | all-to-all | bytes 1179648 | tf_op jit(solution)/shard_map/all_to_all | solution.py:176
  92.7 0.8 copy.14
  (13 shorter events, 0.1 us)
Async XLA Ops:
  0.6 4.5 %slice-start = ((bf16[16,32,1152]{2,1,0:T(8,128)(2,1)}), bf16[15,32,1152]{2,1,0:T(8,128)(2,1)S(1)}, s32[]{:S(2)}) async-start(bf16[16,32,1152]{2,1,0:T(8,128)(2,1)} %param.8), calls=%async_computation.2 | async-start | bytes 2211840 | tf_op jit(solution)/shard_map/slice | solution.py:160
  0.6 4.5 %copy-start.2 = (bf16[32,1152]{1,0:T(8,128)(2,1)S(1)}, bf16[32,1152]{1,0:T(8,128)(2,1)}, u32[]{:S(2)}) copy-start(bf16[32,1152]{1,0:T(8,128)(2,1)} %param.9) | copy-start | bytes 221188
  1.6 8.3 %collective-permute-start = (bf16[1,32,1152]{2,1,0:T(8,128)(2,1)S(1)}, bf16[1,32,1152]{2,1,0:T(8,128)(2,1)S(1)}, u32[]{:S(2)}, u32[]{:S(2)}) collective-permute-start(bf16[1,32,1152]{2,1,0:T(8,128)(2,1)S(1)} %slice.13), channel_id=1, source_target_pairs={{0,32},{32,64},{64,96},{96,128},{128,160},{160,192},{192,224},{224... | collective-permute-start | bytes 221192 | tf_op jit(solution)/shard_map/ppermute | solution.py:21
  10.6 12.2 %copy-start.6 = (s32[16]{0:T(128)S(1)}, s32[16]{0:T(128)}, u32[]{:S(2)}) copy-start(s32[16]{0:T(128)} %param.10) | copy-start | bytes 196
  10.6 12.8 %copy-start.4 = (s32[256]{0:T(256)S(1)}, s32[256]{0:T(256)}, u32[]{:S(2)}) copy-start(s32[256]{0:T(256)} %param.11) | copy-start | bytes 3076
  10.6 14.7 %copy-start = (bf16[1152,576]{0,1:T(8,128)(2,1)S(1)}, bf16[1152,576]{0,1:T(8,128)(2,1)}, u32[]{:S(2)}) copy-start(bf16[1152,576]{0,1:T(8,128)(2,1)} %param.14) | copy-start | bytes 3981316
  10.6 41.4 %all-to-all-start = ((bf16[16,32,1152]{2,1,0:T(8,128)(2,1)}), bf16[16,32,1152]{2,1,0:T(8,128)(2,1)}, u32[]{:S(2)}, u32[]{:S(2)}) async-start(bf16[16,32,1152]{2,1,0:T(8,128)(2,1)} %select_dynamic-update-slice_fusion), calls=%async_computation | async-start | bytes 2359296 | tf_op jit(solution)/shard_map/all_to_all | solution.py:162
  25.4 1.7 %copy-start.1 = (bf16[1152,576]{0,1:T(8,128)(2,1)S(1)}, bf16[1152,576]{0,1:T(8,128)(2,1)}, u32[]{:S(2)}) copy-start(bf16[1152,576]{0,1:T(8,128)(2,1)} %param.15) | copy-start | bytes 3981316
  28.7 5.0 %copy-start.3 = (f32[2,1152]{1,0:T(2,128)S(1)}, f32[2,1152]{1,0:T(2,128)}, u32[]{:S(2)}) copy-start(f32[2,1152]{1,0:T(2,128)} %param.12) | copy-start | bytes 27652
  52.0 7.0 %copy-start.5 = (bf16[1152,576]{0,1:T(8,128)(2,1)S(1)}, bf16[1152,576]{0,1:T(8,128)(2,1)}, u32[]{:S(2)}) copy-start(bf16[1152,576]{0,1:T(8,128)(2,1)} %param.13) | copy-start | bytes 3981316
  57.0 4.9 %collective-permute-start.1 = (bf16[512,1280]{1,0:T(8,128)(2,1)S(1)}, bf16[512,1280]{1,0:T(8,128)(2,1)S(1)}, u32[]{:S(2)}, u32[]{:S(2)}) collective-permute-start(bf16[512,1280]{1,0:T(8,128)(2,1)S(1)} %get-tuple-element.5.own_ref), channel_id=1, source_target_pairs={{0,1},{1,0},{2,3},{3,2},{4,5},{5,4},{6,7},{7,6},{8,9},{9,8},{10,11... | collective-permute-start | bytes 3932168 | tf_op jit(solution)/shard_map/ppermute | solution.py:171

commit v4 on v3

v4 whole, which is shorter than its diff:
```python
import functools
import math

import jax
import jax.numpy as jnp
from jax import lax
from jax.experimental import pallas as pl
from jax.experimental.pallas import tpu as pltpu
from jax.sharding import PartitionSpec as P

HEADS = 8
HD = 72
LANE = 128
WIDTH = HEADS * HD
SHIFT = WIDTH % LANE
SCALE_LOG2 = math.log2(math.e) / math.sqrt(HD)


def from_behind(block, axis, distance):
    devices = range(lax.axis_size(axis))
    route = [(i - distance, i) for i in devices if i - distance in devices]
    return lax.ppermute(block, axis, route)


def modulation(levels, timesteps, mod_table):
    level_count = timesteps.shape[0]
    one_hot = (levels[:, None] == jnp.arange(level_count, dtype=jnp.int32)[None, :]).astype(
        jnp.int32
    )
    noise_time = jnp.sum(one_hot * timesteps[None, :], axis=1).astype(jnp.float32)
    feature_count = mod_table.shape[1]
    frequency = jnp.exp(
        -math.log(10000.0) * jnp.arange(feature_count, dtype=jnp.float32) / feature_count
    )
    phases = noise_time[:, None] * frequency[None, :]
    offset = mod_table[0][None, :] + jnp.cos(phases)
    stretch = mod_table[1][None, :] + jnp.sin(phases)
    return (offset, stretch)


def project_kernel(
    tokens_hbm, stretch_ref, offset_ref, weight_ref, normed_ref, pair_ref, tokens_ref, arrived
):
    rows = tokens_ref.shape[0]
    step = 128
    copies = [
        pltpu.make_async_copy(
            tokens_hbm.at[pl.ds(i * step, step)], tokens_ref.at[pl.ds(i * step, step)], arrived.at[i]
        )
        for i in range(rows // step)
    ]
    for copy in copies:
        copy.start()
    parts = []
    for i in range(rows // step):
        copies[i].wait()
        values = tokens_ref[pl.ds(i * step, step), :].astype(jnp.float32)
        average = jnp.mean(values, axis=-1, keepdims=True)
        centred = values - average
        spread = jnp.mean(centred * centred, axis=-1, keepdims=True)
        normed = centred * lax.rsqrt(spread + 1e-06)
        normed = (normed * (1.0 + stretch_ref[...]) + offset_ref[...]).astype(jnp.bfloat16)
        normed_ref[pl.ds(i * step, step), :] = normed
        parts.append(normed)
    pair_ref[...] = jnp.dot(
        jnp.concatenate(parts, axis=0), weight_ref[...], preferred_element_type=jnp.float32
    ).astype(jnp.bfloat16)


def normalize_and_project(tokens, stretch, offset, weight):
    vmem = pl.BlockSpec(memory_space=pltpu.VMEM)
    rows, width = tokens.shape[0], weight.shape[1]
    return pl.pallas_call(
        project_kernel,
        out_shape=(
            jax.ShapeDtypeStruct(tokens.shape, jnp.bfloat16),
            jax.ShapeDtypeStruct((rows, width), jnp.bfloat16),
        ),
        in_specs=[pl.BlockSpec(memory_space=pl.ANY)] + [vmem] * 3,
        out_specs=(vmem, vmem),
        scratch_shapes=[
            pltpu.VMEM(tokens.shape, jnp.bfloat16),
            pltpu.SemaphoreType.DMA((rows // 128,)),
        ],
        compiler_params=pltpu.CompilerParams(vmem_limit_bytes=24 * 2**20),
        name="project",
    )(tokens, stretch, offset, weight)


def attention_kernel(query_ref, own_ref, other_ref, out_ref):
    dims = (((1,), (1,)), ((), ()))
    window = 2 * LANE
    rows = query_ref.shape[0]
    lane = lax.broadcasted_iota(jnp.int32, (rows, window), 1)
    pairs = (own_ref, other_ref)
    for head in range(HEADS):
        start = min((SHIFT + head * HD) // LANE * LANE, SHIFT + WIDTH - window)
        first = SHIFT + head * HD - start
        inside = (lane >= first) & (lane < first + HD)
        query = jnp.where(inside, query_ref[:, pl.ds(start, window)], 0)
        scores = [
            lax.dot_general(
                query,
                pair[:, pl.ds(WIDTH - SHIFT + start, window)],
                dims,
                preferred_element_type=jnp.float32,
            )
            for pair in pairs
        ]
        peak = jnp.maximum(*(jnp.max(score, axis=1, keepdims=True) for score in scores))
        start = head * HD // LANE * LANE
        first = head * HD - start
        inside = (lane >= first) & (lane < first + HD)
        total = 0.0
        for score, pair in zip(scores, pairs):
            weight = jnp.exp2((score - peak) * SCALE_LOG2).astype(jnp.bfloat16)
            value = jnp.where(inside, pair[:, pl.ds(start, window)], 1)
            total += jnp.dot(weight, value, preferred_element_type=jnp.float32)
        at = first + HD if first + HD < window else 0
        result = total / total[:, at : at + 1]
        if head == 0:
            done = result
        else:
            if start != done_start:
                out_ref[:, pl.ds(done_start, LANE)] = done[:, :LANE].astype(jnp.bfloat16)
                done = jnp.concatenate([done[:, LANE:], result[:, LANE:]], axis=1)
            done = jnp.where(lane < first, done, result)
        done_start = start
    tail = WIDTH - done_start
    out_ref[:, pl.ds(done_start, tail)] = done[:, :tail].astype(jnp.bfloat16)


def attend(query, own, other):
    vmem = pl.BlockSpec(memory_space=pltpu.VMEM)
    rows = query.shape[0]
    return pl.pallas_call(
        attention_kernel,
        out_shape=jax.ShapeDtypeStruct((rows, WIDTH), jnp.bfloat16),
        in_specs=[vmem] * 3,
        out_specs=vmem,
        compiler_params=pltpu.CompilerParams(vmem_limit_bytes=32 * 2**20),
        name="attention",
    )(query, own, other)


def shards(latents, new_frame, levels, timesteps, mod_table, w_query, w_key, w_value):
    frames, tokens_dev, model_width = latents.shape
    groups = lax.axis_size("tok")
    cores = groups // frames
    same_core = [[cores * i + core for i in range(frames)] for core in range(cores)]
    incoming = from_behind(latents[-1:], "band", 1)
    head_frame = jnp.where(lax.axis_index("band") == 0, new_frame[None], incoming)
    moved = lax.optimization_barrier(jnp.concatenate([new_frame[None], latents[:-1]], axis=0))
    queued = lax.dynamic_update_slice_in_dim(moved, head_frame, 0, axis=0)
    mine = lax.all_to_all(
        queued, "tok", split_axis=0, concat_axis=0, axis_index_groups=same_core, tiled=True
    )
    mine = mine.reshape(frames * tokens_dev, model_width)
    level = lax.dynamic_slice_in_dim(levels, lax.axis_index("tok") // cores, 1)
    offset, stretch = modulation(level, timesteps, mod_table)
    w_pair = jnp.concatenate([w_value, w_key], axis=1)
    normed, own = normalize_and_project(mine, stretch, offset, w_pair)
    other = lax.ppermute(own, "tok", [(i, i ^ 1) for i in range(groups)])
    w_shifted = jnp.pad(w_query, ((0, 0), (SHIFT, 0)))
    query = jnp.dot(normed, w_shifted, preferred_element_type=jnp.float32).astype(jnp.bfloat16)
    result = attend(query, own, other)
    attended = lax.all_to_all(
        result.reshape(frames, tokens_dev, WIDTH),
        "tok",
        split_axis=0,
        concat_axis=0,
        axis_index_groups=same_core,
        tiled=True,
    )
    return (queued, attended)


def solution(mesh):
    in_specs = (P("band", "tok", None), P("tok", None), P("band"), P(), P(), P(), P(), P())
    out_specs = (P("band", "tok", None), P("band", "tok", None))
    return jax.shard_map(shards, mesh=mesh, in_specs=in_specs, out_specs=out_specs, check_vma=False)
```

time: 94 us -> 92.4 us (0.983)
  local copies, waits for them, and re-layouts: 10.8 us -> 5.74 us
  other arithmetic: 3.26 us -> 5.92 us
  waiting for transfers between devices: 23.6 us -> 25.8 us
  Pallas kernels: 10.8 us -> 9.65 us
    concatenate x1 -> x0, local copies, waits for them, and re-layouts: 4.98 us -> none  [shards(): w_pair = jnp.concatenate([w_key, gap, w_value, gap], axis=1)]
    concatenate x0 -> x1, other arithmetic: none -> 2.67 us  [shards(): w_pair = jnp.concatenate([w_value, w_key], axis=1)]
    all_to_all x1, waiting for transfers between devices: 18.1 us -> 20.5 us  [shards(): lax.all_to_all(queued, 'tok', split_axis=0, concat_axis=0, axis_index_gro...]
    pallas_call x1, Pallas kernels: 5.05 us -> 3.88 us  [normalize_and_project(): pl.pallas_call(project_kernel, out_shape=(jax.ShapeDtypeStruct(tokens.sha...]
  transfers between devices with their start and end apart: 3 -> 3, of which waited for: 3 -> 3; matrix products, arithmetic and copies ran while one was open for 14% -> 11% of each run, Pallas kernels for 0% -> 0%
where the time goes in v4:
time: 92.4 us; the launch traced here: 92.1 us
  waiting for transfers between devices  25.8 us (28%)
  blocking collectives  25 us (27%)
  starting transfers between devices  17.4 us (19%)
  Pallas kernels  9.65 us (10%)
  other arithmetic  5.92 us (6%)
  local copies, waits for them, and re-layouts  5.74 us (6%)
  between operations  1.41 us (2%)
  matrix products  1.19 us (1%)
    all_to_all x1, blocking collectives, shards(): lax.all_to_all(result.reshape(frames, tokens_dev, WIDTH), 'tok', split_ax...  25 us
    all_to_all x1, waiting for transfers between devices, shards(): lax.all_to_all(queued, 'tok', split_axis=0, concat_axis=0, axis_index_gro...  20.5 us
    all_to_all x1, starting transfers between devices, shards(): lax.all_to_all(queued, 'tok', split_axis=0, concat_axis=0, axis_index_gro...  12 us
    pallas_call x1, Pallas kernels, attend(): pl.pallas_call(attention_kernel, out_shape=jax.ShapeDtypeStruct((rows, WI...  5.77 us
    unnamed x17, local copies, waits for them, and re-layouts  4.16 us
    pallas_call x1, Pallas kernels, normalize_and_project(): pl.pallas_call(project_kernel, out_shape=(jax.ShapeDtypeStruct(tokens.sha...  3.88 us
    ppermute x1, waiting for transfers between devices, from_behind(): return lax.ppermute(block, axis, route)  3.7 us
    ppermute x1, starting transfers between devices, from_behind(): return lax.ppermute(block, axis, route)  3.47 us
  transfers between devices with their start and end apart: 3, of which 3 were waited for; matrix products, arithmetic and copies ran while one was open for 11% of the time, Pallas kernels for 0%

profile of v4, /device:TPU:64, one launch (start us, length us, event | category | flops | bytes accessed | tf_op | source)
XLA Modules:
  0.0 92.1 jit_solution(18367709013224960480)
XLA Ops:
  0.6 0.0 slice-start
  0.6 0.0 copy-start.2
  0.6 1.0 %slice.13 = bf16[1,32,1152]{2,1,0:T(8,128)(2,1)S(1)} slice(bf16[16,32,1152]{2,1,0:T(8,128)(2,1)} %param.8), slice={[15:16], [0:32], [0:1152]} | slice | bytes 147456 | tf_op jit(solution)/shard_map/slice | solution.py:151
  1.6 3.5 %collective-permute-start = (bf16[1,32,1152]{2,1,0:T(8,128)(2,1)S(1)}, bf16[1,32,1152]{2,1,0:T(8,128)(2,1)S(1)}, u32[]{:S(2)}, u32[]{:S(2)}) collective-permute-start(bf16[1,32,1152]{2,1,0:T(8,128)(2,1)S(1)} %slice.13), channel_id=1, source_target_pairs={{0,32},{32,64},{64,96},{96,128},{128,160},{160,192},{192,224},{224... | collective-permute-start | bytes 221192 | tf_op jit(solution)/shard_map/ppermute | solution.py:22
  5.1 1.1 %pad_maximum_fusion.1 = bf16[16,32,1152]{2,1,0:T(8,128)(2,1)} fusion(bf16[15,32,1152]{2,1,0:T(8,128)(2,1)S(1)} %slice-done, bf16[1,32,1152]{2,1,0:T(8,128)(2,1)S(1)} %bitcast.7), kind=kLoop, calls=%fused_computation.4 | loop fusion | flops 589824 | bytes 2359296 | tf_op jit(solution)/shard_map/concatenate | solution.py:153
  6.3 3.7 %collective-permute-done = bf16[1,32,1152]{2,1,0:T(8,128)(2,1)S(1)} collective-permute-done((bf16[1,32,1152]{2,1,0:T(8,128)(2,1)S(1)}, bf16[1,32,1152]{2,1,0:T(8,128)(2,1)S(1)}, u32[]{:S(2)}, u32[]{:S(2)}) %collective-permute-start) | collective-permute-done | bytes 73760 | tf_op jit(solution)/shard_map/ppermute | solution.py:22
  10.0 0.7 select_dynamic-update-slice_fusion
  10.6 12.0 %all-to-all-start = ((bf16[16,32,1152]{2,1,0:T(8,128)(2,1)}), bf16[16,32,1152]{2,1,0:T(8,128)(2,1)}, u32[]{:S(2)}, u32[]{:S(2)}) async-start(bf16[16,32,1152]{2,1,0:T(8,128)(2,1)} %select_dynamic-update-slice_fusion), calls=%async_computation | async-start | bytes 2359296 | tf_op jit(solution)/shard_map/all_to_all | solution.py:155
  22.7 0.0 copy-done.6
  22.7 0.6 dynamic_slice.3
  23.3 1.3 %fusion.5 = s32[]{:T(128)} fusion(s32[256]{0:T(256)S(1)} %copy-done.4, s32[]{:T(128)} %bitcast.2), kind=kLoop, calls=%fused_computation.10 | loop fusion | flops 767 | bytes 1032 | tf_op jit(solution)/shard_map/reduce_sum | solution.py:30
  25.2 0.0 copy-start.1
  25.2 1.7 %copy.11 = bf16[1152,576]{1,0:T(8,128)(2,1)} copy(bf16[1152,576]{0,1:T(8,128)(2,1)S(1)} %copy-done) | data formatting | bytes 2654208 | tf_op args[6]
  26.9 1.6 %copy.10 = bf16[1152,576]{1,0:T(8,128)(2,1)} copy(bf16[1152,576]{0,1:T(8,128)(2,1)S(1)} %copy-done.1) | data formatting | bytes 2654208 | tf_op args[7]
  28.5 0.2 cosine_add_fusion
  28.7 2.7 %pad_maximum_fusion.weight_ref = bf16[1152,1152]{1,0:T(8,128)(2,1)S(1)} fusion(bf16[1152,576]{1,0:T(8,128)(2,1)} %copy.11, bf16[1152,576]{1,0:T(8,128)(2,1)} %copy.10), kind=kLoop, calls=%fused_computation | loop fusion | flops 5308416 | bytes 5308416 | tf_op jit(solution)/shard_map/concatenate | solution.py:161
  31.4 20.5 %all-to-all-done = bf16[16,32,1152]{2,1,0:T(8,128)(2,1)} async-done(((bf16[16,32,1152]{2,1,0:T(8,128)(2,1)}), bf16[16,32,1152]{2,1,0:T(8,128)(2,1)}, u32[]{:S(2)}, u32[]{:S(2)}) %all-to-all-start) | async-done | bytes 1179680 | tf_op jit(solution)/shard_map/all_to_all | solution.py:155
  51.9 3.9 %project.1 = (bf16[512,1152]{1,0:T(8,128)(2,1)S(1)}, bf16[512,1152]{1,0:T(8,128)(2,1)S(1)}) custom-call(bf16[512,1152]{1,0:T(8,128)(2,1)} %bitcast.1.tokens_hbm, f32[1,1152]{1,0:T(1,128)S(1)} %get-tuple-element.7.stretch_ref, f32[1,1152]{1,0:T(1,128)S(1)} %get-tuple-element.6.offset_ref, bf16[1152,1152]{1,0:T(8,128)(2,1)S(1)} %pad_maximum_fusion.weight_ref), custom_call_target="tpu_custom_call" | custom-call | tf_op jit(solution)/shard_map/project/pallas_call | solution.py:73
  55.7 1.9 %collective-permute-start.1 = (bf16[512,1152]{1,0:T(8,128)(2,1)S(1)}, bf16[512,1152]{1,0:T(8,128)(2,1)S(1)}, u32[]{:S(2)}, u32[]{:S(2)}) collective-permute-start(bf16[512,1152]{1,0:T(8,128)(2,1)S(1)} %get-tuple-element.5.own_ref), channel_id=1, source_target_pairs={{0,1},{1,0},{2,3},{3,2},{4,5},{5,4},{6,7},{7,6},{8,9},{9,8},{10,11... | collective-permute-start | bytes 3538952 | tf_op jit(solution)/shard_map/ppermute | solution.py:163
  57.7 1.2 %fusion.2.query_ref = bf16[512,640]{1,0:T(8,128)(2,1)S(1)} fusion(bf16[512,1152]{1,0:T(8,128)(2,1)S(1)} %get-tuple-element.4, bf16[1152,576]{0,1:T(8,128)(2,1)S(1)} %copy-done.5), kind=kOutput, calls=%fused_computation.3 | convolution fusion | flops 755302400 | bytes 3162112 | tf_op jit(solution)/shard_map/dot_general | solution.py:165
  58.9 1.6 %collective-permute-done.1.other_ref = bf16[512,1152]{1,0:T(8,128)(2,1)S(1)} collective-permute-done((bf16[512,1152]{1,0:T(8,128)(2,1)S(1)}, bf16[512,1152]{1,0:T(8,128)(2,1)S(1)}, u32[]{:S(2)}, u32[]{:S(2)}) %collective-permute-start.1) | collective-permute-done | bytes 1179680 | tf_op jit(solution)/shard_map/ppermute | solution.py:163
  60.5 5.8 %attention.1 = bf16[512,576]{1,0:T(8,128)(2,1)S(1)} custom-call(bf16[512,640]{1,0:T(8,128)(2,1)S(1)} %fusion.2.query_ref, bf16[512,1152]{1,0:T(8,128)(2,1)S(1)} %get-tuple-element.5.own_ref, bf16[512,1152]{1,0:T(8,128)(2,1)S(1)} %collective-permute-done.1.other_ref), custom_call_target="tpu_custom_call" | custom-call | tf_op jit(solution)/shard_map/attention/pallas_call | solution.py:136
  66.3 25.0 %all_to_all.10 = bf16[16,32,576]{2,1,0:T(8,128)(2,1)S(1)} all-to-all(bf16[16,32,576]{2,1,0:T(8,128)(2,1)S(1)} %bitcast.6), channel_id=1, replica_groups={{0,2,4,6,8,10,12,14,16,18,20,22,24,26,28,30},{1,3,5,7,9,11,13,15,17,19,..., dimensions={0} | all-to-all | bytes 1179648 | tf_op jit(solution)/shard_map/all_to_all | solution.py:167
  91.2 0.8 copy.14
  (12 shorter events, 0.0 us)
Async XLA Ops:
  0.6 4.5 %slice-start = ((bf16[16,32,1152]{2,1,0:T(8,128)(2,1)}), bf16[15,32,1152]{2,1,0:T(8,128)(2,1)S(1)}, s32[]{:S(2)}) async-start(bf16[16,32,1152]{2,1,0:T(8,128)(2,1)} %param.8), calls=%async_computation.2 | async-start | bytes 2211840 | tf_op jit(solution)/shard_map/slice | solution.py:153
  0.6 4.5 %copy-start.2 = (bf16[32,1152]{1,0:T(8,128)(2,1)S(1)}, bf16[32,1152]{1,0:T(8,128)(2,1)}, u32[]{:S(2)}) copy-start(bf16[32,1152]{1,0:T(8,128)(2,1)} %param.9) | copy-start | bytes 221188
  1.6 8.3 %collective-permute-start = (bf16[1,32,1152]{2,1,0:T(8,128)(2,1)S(1)}, bf16[1,32,1152]{2,1,0:T(8,128)(2,1)S(1)}, u32[]{:S(2)}, u32[]{:S(2)}) collective-permute-start(bf16[1,32,1152]{2,1,0:T(8,128)(2,1)S(1)} %slice.13), channel_id=1, source_target_pairs={{0,32},{32,64},{64,96},{96,128},{128,160},{160,192},{192,224},{224... | collective-permute-start | bytes 221192 | tf_op jit(solution)/shard_map/ppermute | solution.py:22
  6.3 16.4 %copy-start.6 = (s32[16]{0:T(128)S(1)}, s32[16]{0:T(128)}, u32[]{:S(2)}) copy-start(s32[16]{0:T(128)} %param.10) | copy-start | bytes 196
  6.3 17.0 %copy-start.4 = (s32[256]{0:T(256)S(1)}, s32[256]{0:T(256)}, u32[]{:S(2)}) copy-start(s32[256]{0:T(256)} %param.11) | copy-start | bytes 3076
  6.3 18.9 %copy-start = (bf16[1152,576]{0,1:T(8,128)(2,1)S(1)}, bf16[1152,576]{0,1:T(8,128)(2,1)}, u32[]{:S(2)}) copy-start(bf16[1152,576]{0,1:T(8,128)(2,1)} %param.14) | copy-start | bytes 3981316
  10.6 41.2 %all-to-all-start = ((bf16[16,32,1152]{2,1,0:T(8,128)(2,1)}), bf16[16,32,1152]{2,1,0:T(8,128)(2,1)}, u32[]{:S(2)}, u32[]{:S(2)}) async-start(bf16[16,32,1152]{2,1,0:T(8,128)(2,1)} %select_dynamic-update-slice_fusion), calls=%async_computation | async-start | bytes 2359296 | tf_op jit(solution)/shard_map/all_to_all | solution.py:155
  25.2 1.7 %copy-start.1 = (bf16[1152,576]{0,1:T(8,128)(2,1)S(1)}, bf16[1152,576]{0,1:T(8,128)(2,1)}, u32[]{:S(2)}) copy-start(bf16[1152,576]{0,1:T(8,128)(2,1)} %param.15) | copy-start | bytes 3981316
  26.9 1.6 %copy-start.3 = (f32[2,1152]{1,0:T(2,128)S(1)}, f32[2,1152]{1,0:T(2,128)}, u32[]{:S(2)}) copy-start(f32[2,1152]{1,0:T(2,128)} %param.12) | copy-start | bytes 27652
  51.9 5.8 %copy-start.5 = (bf16[1152,576]{0,1:T(8,128)(2,1)S(1)}, bf16[1152,576]{0,1:T(8,128)(2,1)}, u32[]{:S(2)}) copy-start(bf16[1152,576]{0,1:T(8,128)(2,1)} %param.13) | copy-start | bytes 3981316
  55.7 4.7 %collective-permute-start.1 = (bf16[512,1152]{1,0:T(8,128)(2,1)S(1)}, bf16[512,1152]{1,0:T(8,128)(2,1)S(1)}, u32[]{:S(2)}, u32[]{:S(2)}) collective-permute-start(bf16[512,1152]{1,0:T(8,128)(2,1)S(1)} %get-tuple-element.5.own_ref), channel_id=1, source_target_pairs={{0,1},{1,0},{2,3},{3,2},{4,5},{5,4},{6,7},{7,6},{8,9},{9,8},{10,11... | collective-permute-start | bytes 3538952 | tf_op jit(solution)/shard_map/ppermute | solution.py:163

commit v5 on v4

--- a/solution.py
+++ b/solution.py
@@ -13,6 +13,7 @@
 LANE = 128
 WIDTH = HEADS * HD
 SHIFT = WIDTH % LANE
+OWNERS = (15, 1, 14, 0, 4, 8, 9, 2, 5, 7, 12, 10, 3, 13, 11, 6)
 SCALE_LOG2 = math.log2(math.e) / math.sqrt(HD)
 
 
@@ -147,7 +148,7 @@
     frames, tokens_dev, model_width = latents.shape
     groups = lax.axis_size("tok")
     cores = groups // frames
-    same_core = [[cores * i + core for i in range(frames)] for core in range(cores)]
+    same_core = [[cores * chip + core for chip in OWNERS] for core in range(cores)]
     incoming = from_behind(latents[-1:], "band", 1)
     head_frame = jnp.where(lax.axis_index("band") == 0, new_frame[None], incoming)
     moved = lax.optimization_barrier(jnp.concatenate([new_frame[None], latents[:-1]], axis=0))
@@ -156,7 +157,8 @@
         queued, "tok", split_axis=0, concat_axis=0, axis_index_groups=same_core, tiled=True
     )
     mine = mine.reshape(frames * tokens_dev, model_width)
-    level = lax.dynamic_slice_in_dim(levels, lax.axis_index("tok") // cores, 1)
+    chip = lax.axis_index("tok") // cores
+    level = jnp.sum(jnp.where(jnp.array(OWNERS) == chip, levels, 0), keepdims=True)
     offset, stretch = modulation(level, timesteps, mod_table)
     w_pair = jnp.concatenate([w_value, w_key], axis=1)
     normed, own = normalize_and_project(mine, stretch, offset, w_pair)

time: 92.4 us -> 93.2 us (level)
  the two profiles are of different devices: /device:TPU:64 before, /device:TPU:38 now
where the time goes in v5:
time: 93.2 us; the launch traced here: 92.9 us
  blocking collectives  25.9 us (28%)
  waiting for transfers between devices  25.4 us (27%)
  starting transfers between devices  17.7 us (19%)
  Pallas kernels  9.65 us (10%)
  other arithmetic  6.56 us (7%)
  local copies, waits for them, and re-layouts  5.17 us (6%)
  between operations  1.4 us (2%)
  matrix products  1.18 us (1%)
    all_to_all x1, blocking collectives, shards(): lax.all_to_all(result.reshape(frames, tokens_dev, WIDTH), 'tok', split_ax...  25.9 us
    all_to_all x1, waiting for transfers between devices, shards(): lax.all_to_all(queued, 'tok', split_axis=0, concat_axis=0, axis_index_gro...  20.1 us
    all_to_all x1, starting transfers between devices, shards(): lax.all_to_all(queued, 'tok', split_axis=0, concat_axis=0, axis_index_gro...  13.2 us
    pallas_call x1, Pallas kernels, attend(): pl.pallas_call(attention_kernel, out_shape=jax.ShapeDtypeStruct((rows, WI...  5.77 us
    unnamed x19, local copies, waits for them, and re-layouts  4.18 us
    pallas_call x1, Pallas kernels, normalize_and_project(): pl.pallas_call(project_kernel, out_shape=(jax.ShapeDtypeStruct(tokens.sha...  3.88 us
    ppermute x1, waiting for transfers between devices, from_behind(): return lax.ppermute(block, axis, route)  3.69 us
    concatenate x1, other arithmetic, shards(): w_pair = jnp.concatenate([w_value, w_key], axis=1)  2.67 us
  transfers between devices with their start and end apart: 3, of which 3 were waited for; matrix products, arithmetic and copies ran while one was open for 11% of the time, Pallas kernels for 0%

profile of v5, /device:TPU:38, one launch (start us, length us, event | category | flops | bytes accessed | tf_op | source)
XLA Modules:
  0.0 92.9 jit_solution(1820887042616513669)
XLA Ops:
  0.6 0.0 slice-start
  0.6 0.0 copy-start.2
  0.6 1.0 %slice.13 = bf16[1,32,1152]{2,1,0:T(8,128)(2,1)S(1)} slice(bf16[16,32,1152]{2,1,0:T(8,128)(2,1)} %param.9), slice={[15:16], [0:32], [0:1152]} | slice | bytes 147456 | tf_op jit(solution)/shard_map/slice | solution.py:152
  1.6 2.6 %collective-permute-start = (bf16[1,32,1152]{2,1,0:T(8,128)(2,1)S(1)}, bf16[1,32,1152]{2,1,0:T(8,128)(2,1)S(1)}, u32[]{:S(2)}, u32[]{:S(2)}) collective-permute-start(bf16[1,32,1152]{2,1,0:T(8,128)(2,1)S(1)} %slice.13), channel_id=1, source_target_pairs={{0,32},{32,64},{64,96},{96,128},{128,160},{160,192},{192,224},{224... | collective-permute-start | bytes 221192 | tf_op jit(solution)/shard_map/ppermute | solution.py:23
  4.2 1.1 %pad_maximum_fusion.1 = bf16[16,32,1152]{2,1,0:T(8,128)(2,1)} fusion(bf16[15,32,1152]{2,1,0:T(8,128)(2,1)S(1)} %slice-done, bf16[1,32,1152]{2,1,0:T(8,128)(2,1)S(1)} %bitcast.6), kind=kLoop, calls=%fused_computation.4 | loop fusion | flops 589824 | bytes 2359296 | tf_op jit(solution)/shard_map/concatenate | solution.py:154
  5.4 3.7 %collective-permute-done = bf16[1,32,1152]{2,1,0:T(8,128)(2,1)S(1)} collective-permute-done((bf16[1,32,1152]{2,1,0:T(8,128)(2,1)S(1)}, bf16[1,32,1152]{2,1,0:T(8,128)(2,1)S(1)}, u32[]{:S(2)}, u32[]{:S(2)}) %collective-permute-start) | collective-permute-done | bytes 73760 | tf_op jit(solution)/shard_map/ppermute | solution.py:23
  9.1 0.7 select_dynamic-update-slice_fusion
  9.7 13.2 %all-to-all-start = ((bf16[16,32,1152]{2,1,0:T(8,128)(2,1)}), bf16[16,32,1152]{2,1,0:T(8,128)(2,1)}, u32[]{:S(2)}, u32[]{:S(2)}) async-start(bf16[16,32,1152]{2,1,0:T(8,128)(2,1)} %select_dynamic-update-slice_fusion), calls=%async_computation | async-start | bytes 2359296 | tf_op jit(solution)/shard_map/all_to_all | solution.py:156
  23.0 0.6 fusion.6
  23.6 0.0 copy-done.4
  23.6 1.3 %fusion.5 = s32[]{:T(128)} fusion(s32[256]{0:T(256)S(1)} %copy-done.4, s32[]{:T(128)} %fusion.6), kind=kLoop, calls=%fused_computation.11 | loop fusion | flops 767 | bytes 1032 | tf_op jit(solution)/shard_map/reduce_sum | solution.py:31
  25.5 0.0 copy-start.1
  25.6 1.7 %copy.12 = bf16[1152,576]{1,0:T(8,128)(2,1)} copy(bf16[1152,576]{0,1:T(8,128)(2,1)S(1)} %copy-done) | data formatting | bytes 2654208 | tf_op args[6]
  27.2 1.6 %copy.11 = bf16[1152,576]{1,0:T(8,128)(2,1)} copy(bf16[1152,576]{0,1:T(8,128)(2,1)S(1)} %copy-done.1) | data formatting | bytes 2654208 | tf_op args[7]
  28.9 0.2 cosine_add_fusion
  29.0 2.7 %pad_maximum_fusion.weight_ref = bf16[1152,1152]{1,0:T(8,128)(2,1)S(1)} fusion(bf16[1152,576]{1,0:T(8,128)(2,1)} %copy.12, bf16[1152,576]{1,0:T(8,128)(2,1)} %copy.11), kind=kLoop, calls=%fused_computation | loop fusion | flops 5308416 | bytes 5308416 | tf_op jit(solution)/shard_map/concatenate | solution.py:163
  31.7 20.1 %all-to-all-done = bf16[16,32,1152]{2,1,0:T(8,128)(2,1)} async-done(((bf16[16,32,1152]{2,1,0:T(8,128)(2,1)}), bf16[16,32,1152]{2,1,0:T(8,128)(2,1)}, u32[]{:S(2)}, u32[]{:S(2)}) %all-to-all-start) | async-done | bytes 1179680 | tf_op jit(solution)/shard_map/all_to_all | solution.py:156
  51.8 3.9 %project.1 = (bf16[512,1152]{1,0:T(8,128)(2,1)S(1)}, bf16[512,1152]{1,0:T(8,128)(2,1)S(1)}) custom-call(bf16[512,1152]{1,0:T(8,128)(2,1)} %bitcast.1.tokens_hbm, f32[1,1152]{1,0:T(1,128)S(1)} %get-tuple-element.7.stretch_ref, f32[1,1152]{1,0:T(1,128)S(1)} %get-tuple-element.6.offset_ref, bf16[1152,1152]{1,0:T(8,128)(2,1)S(1)} %pad_maximum_fusion.weight_ref), custom_call_target="tpu_custom_call" | custom-call | tf_op jit(solution)/shard_map/project/pallas_call | solution.py:74
  55.7 1.9 %collective-permute-start.1 = (bf16[512,1152]{1,0:T(8,128)(2,1)S(1)}, bf16[512,1152]{1,0:T(8,128)(2,1)S(1)}, u32[]{:S(2)}, u32[]{:S(2)}) collective-permute-start(bf16[512,1152]{1,0:T(8,128)(2,1)S(1)} %get-tuple-element.5.own_ref), channel_id=1, source_target_pairs={{0,1},{1,0},{2,3},{3,2},{4,5},{5,4},{6,7},{7,6},{8,9},{9,8},{10,11... | collective-permute-start | bytes 3538952 | tf_op jit(solution)/shard_map/ppermute | solution.py:165
  57.6 1.2 %fusion.2.query_ref = bf16[512,640]{1,0:T(8,128)(2,1)S(1)} fusion(bf16[512,1152]{1,0:T(8,128)(2,1)S(1)} %get-tuple-element.4, bf16[1152,576]{0,1:T(8,128)(2,1)S(1)} %copy-done.7), kind=kOutput, calls=%fused_computation.3 | convolution fusion | flops 755302400 | bytes 3162112 | tf_op jit(solution)/shard_map/dot_general | solution.py:167
  58.8 1.6 %collective-permute-done.1.other_ref = bf16[512,1152]{1,0:T(8,128)(2,1)S(1)} collective-permute-done((bf16[512,1152]{1,0:T(8,128)(2,1)S(1)}, bf16[512,1152]{1,0:T(8,128)(2,1)S(1)}, u32[]{:S(2)}, u32[]{:S(2)}) %collective-permute-start.1) | collective-permute-done | bytes 1179680 | tf_op jit(solution)/shard_map/ppermute | solution.py:165
  60.4 5.8 %attention.1 = bf16[512,576]{1,0:T(8,128)(2,1)S(1)} custom-call(bf16[512,640]{1,0:T(8,128)(2,1)S(1)} %fusion.2.query_ref, bf16[512,1152]{1,0:T(8,128)(2,1)S(1)} %get-tuple-element.5.own_ref, bf16[512,1152]{1,0:T(8,128)(2,1)S(1)} %collective-permute-done.1.other_ref), custom_call_target="tpu_custom_call" | custom-call | tf_op jit(solution)/shard_map/attention/pallas_call | solution.py:137
  66.2 25.9 %all_to_all.10 = bf16[16,32,576]{2,1,0:T(8,128)(2,1)S(1)} all-to-all(bf16[16,32,576]{2,1,0:T(8,128)(2,1)S(1)} %bitcast.5), channel_id=1, replica_groups={{30,2,28,0,8,16,18,4,10,14,24,20,6,26,22,12},{31,3,29,1,9,17,19,5,11,15..., dimensions={0} | all-to-all | bytes 1179648 | tf_op jit(solution)/shard_map/all_to_all | solution.py:169
  92.0 0.8 copy.15
  (14 shorter events, 0.0 us)
Async XLA Ops:
  0.6 3.6 %slice-start = ((bf16[16,32,1152]{2,1,0:T(8,128)(2,1)}), bf16[15,32,1152]{2,1,0:T(8,128)(2,1)S(1)}, s32[]{:S(2)}) async-start(bf16[16,32,1152]{2,1,0:T(8,128)(2,1)} %param.9), calls=%async_computation.2 | async-start | bytes 2211840 | tf_op jit(solution)/shard_map/slice | solution.py:154
  0.6 3.6 %copy-start.2 = (bf16[32,1152]{1,0:T(8,128)(2,1)S(1)}, bf16[32,1152]{1,0:T(8,128)(2,1)}, u32[]{:S(2)}) copy-start(bf16[32,1152]{1,0:T(8,128)(2,1)} %param.10) | copy-start | bytes 221188
  1.6 7.4 %collective-permute-start = (bf16[1,32,1152]{2,1,0:T(8,128)(2,1)S(1)}, bf16[1,32,1152]{2,1,0:T(8,128)(2,1)S(1)}, u32[]{:S(2)}, u32[]{:S(2)}) collective-permute-start(bf16[1,32,1152]{2,1,0:T(8,128)(2,1)S(1)} %slice.13), channel_id=1, source_target_pairs={{0,32},{32,64},{64,96},{96,128},{128,160},{160,192},{192,224},{224... | collective-permute-start | bytes 221192 | tf_op jit(solution)/shard_map/ppermute | solution.py:23
  5.4 17.6 %copy-start.5 = (s32[16]{0:T(128)S(1)}, s32[16]{0:T(128)}, u32[]{:S(2)}) copy-start(s32[16]{0:T(128)} %param.11) | copy-start | bytes 196
  5.4 17.6 %copy-start.6 = (s32[16]{0:T(128)S(1)}, s32[16]{0:T(128)}, u32[]{:S(2)}) copy-start(s32[16]{0:T(128)} %constant.35.clone) | copy-start | bytes 196
  5.4 18.2 %copy-start.4 = (s32[256]{0:T(256)S(1)}, s32[256]{0:T(256)}, u32[]{:S(2)}) copy-start(s32[256]{0:T(256)} %param.12) | copy-start | bytes 3076
  5.4 20.2 %copy-start = (bf16[1152,576]{0,1:T(8,128)(2,1)S(1)}, bf16[1152,576]{0,1:T(8,128)(2,1)}, u32[]{:S(2)}) copy-start(bf16[1152,576]{0,1:T(8,128)(2,1)} %param.15) | copy-start | bytes 3981316
  9.7 42.1 %all-to-all-start = ((bf16[16,32,1152]{2,1,0:T(8,128)(2,1)}), bf16[16,32,1152]{2,1,0:T(8,128)(2,1)}, u32[]{:S(2)}, u32[]{:S(2)}) async-start(bf16[16,32,1152]{2,1,0:T(8,128)(2,1)} %select_dynamic-update-slice_fusion), calls=%async_computation | async-start | bytes 2359296 | tf_op jit(solution)/shard_map/all_to_all | solution.py:156
  25.5 1.7 %copy-start.1 = (bf16[1152,576]{0,1:T(8,128)(2,1)S(1)}, bf16[1152,576]{0,1:T(8,128)(2,1)}, u32[]{:S(2)}) copy-start(bf16[1152,576]{0,1:T(8,128)(2,1)} %param.16) | copy-start | bytes 3981316
  27.2 1.7 %copy-start.3 = (f32[2,1152]{1,0:T(2,128)S(1)}, f32[2,1152]{1,0:T(2,128)}, u32[]{:S(2)}) copy-start(f32[2,1152]{1,0:T(2,128)} %param.13) | copy-start | bytes 27652
  51.8 5.8 %copy-start.7 = (bf16[1152,576]{0,1:T(8,128)(2,1)S(1)}, bf16[1152,576]{0,1:T(8,128)(2,1)}, u32[]{:S(2)}) copy-start(bf16[1152,576]{0,1:T(8,128)(2,1)} %param.14) | copy-start | bytes 3981316
  55.7 4.7 %collective-permute-start.1 = (bf16[512,1152]{1,0:T(8,128)(2,1)S(1)}, bf16[512,1152]{1,0:T(8,128)(2,1)S(1)}, u32[]{:S(2)}, u32[]{:S(2)}) collective-permute-start(bf16[512,1152]{1,0:T(8,128)(2,1)S(1)} %get-tuple-element.5.own_ref), channel_id=1, source_target_pairs={{0,1},{1,0},{2,3},{3,2},{4,5},{5,4},{6,7},{7,6},{8,9},{9,8},{10,11... | collective-permute-start | bytes 3538952 | tf_op jit(solution)/shard_map/ppermute | solution.py:165

commit v6 on v5

--- a/solution.py
+++ b/solution.py
@@ -13,7 +13,7 @@
 LANE = 128
 WIDTH = HEADS * HD
 SHIFT = WIDTH % LANE
-OWNERS = (15, 1, 14, 0, 4, 8, 9, 2, 5, 7, 12, 10, 3, 13, 11, 6)
+OWNERS = (10, 11, 8, 13, 14, 0, 9, 7, 6, 15, 1, 3, 2, 12, 4, 5)
 SCALE_LOG2 = math.log2(math.e) / math.sqrt(HD)
 
 

time: 93.2 us -> 90.6 us (0.972)
  the two profiles are of different devices: /device:TPU:38 before, /device:TPU:56 now
where the time goes in v6:
time: 90.6 us; the launch traced here: 89 us
  blocking collectives  31.3 us (35%)
  starting transfers between devices  21.2 us (23%)
  waiting for transfers between devices  12.6 us (14%)
  Pallas kernels  9.65 us (11%)
  other arithmetic  6.56 us (7%)
  local copies, waits for them, and re-layouts  5.17 us (6%)
  between operations  1.4 us (2%)
  matrix products  1.19 us (1%)
    all_to_all x1, blocking collectives, shards(): lax.all_to_all(result.reshape(frames, tokens_dev, WIDTH), 'tok', split_ax...  31.3 us
    all_to_all x1, starting transfers between devices, shards(): lax.all_to_all(queued, 'tok', split_axis=0, concat_axis=0, axis_index_gro...  15.8 us
    all_to_all x1, waiting for transfers between devices, shards(): lax.all_to_all(queued, 'tok', split_axis=0, concat_axis=0, axis_index_gro...  9.42 us
    pallas_call x1, Pallas kernels, attend(): pl.pallas_call(attention_kernel, out_shape=jax.ShapeDtypeStruct((rows, WI...  5.77 us
    unnamed x19, local copies, waits for them, and re-layouts  4.18 us
    pallas_call x1, Pallas kernels, normalize_and_project(): pl.pallas_call(project_kernel, out_shape=(jax.ShapeDtypeStruct(tokens.sha...  3.88 us
    ppermute x1, starting transfers between devices, from_behind(): return lax.ppermute(block, axis, route)  3.47 us
    concatenate x1, other arithmetic, shards(): w_pair = jnp.concatenate([w_value, w_key], axis=1)  2.67 us
  transfers between devices with their start and end apart: 3, of which 3 were waited for; matrix products, arithmetic and copies ran while one was open for 12% of the time, Pallas kernels for 0%

profile of v6, /device:TPU:56, one launch (start us, length us, event | category | flops | bytes accessed | tf_op | source)
XLA Modules:
  0.0 89.0 jit_solution(10043580707802906278)
XLA Ops:
  0.6 0.0 slice-start
  0.6 0.0 copy-start.2
  0.6 1.0 %slice.13 = bf16[1,32,1152]{2,1,0:T(8,128)(2,1)S(1)} slice(bf16[16,32,1152]{2,1,0:T(8,128)(2,1)} %param.9), slice={[15:16], [0:32], [0:1152]} | slice | bytes 147456 | tf_op jit(solution)/shard_map/slice | solution.py:152
  1.6 3.5 %collective-permute-start = (bf16[1,32,1152]{2,1,0:T(8,128)(2,1)S(1)}, bf16[1,32,1152]{2,1,0:T(8,128)(2,1)S(1)}, u32[]{:S(2)}, u32[]{:S(2)}) collective-permute-start(bf16[1,32,1152]{2,1,0:T(8,128)(2,1)S(1)} %slice.13), channel_id=1, source_target_pairs={{0,32},{32,64},{64,96},{96,128},{128,160},{160,192},{192,224},{224... | collective-permute-start | bytes 221192 | tf_op jit(solution)/shard_map/ppermute | solution.py:23
  5.1 0.0 slice-done
  5.1 1.1 %pad_maximum_fusion.1 = bf16[16,32,1152]{2,1,0:T(8,128)(2,1)} fusion(bf16[15,32,1152]{2,1,0:T(8,128)(2,1)S(1)} %slice-done, bf16[1,32,1152]{2,1,0:T(8,128)(2,1)S(1)} %bitcast.6), kind=kLoop, calls=%fused_computation.4 | loop fusion | flops 589824 | bytes 2359296 | tf_op jit(solution)/shard_map/concatenate | solution.py:154
  6.3 1.6 %collective-permute-done = bf16[1,32,1152]{2,1,0:T(8,128)(2,1)S(1)} collective-permute-done((bf16[1,32,1152]{2,1,0:T(8,128)(2,1)S(1)}, bf16[1,32,1152]{2,1,0:T(8,128)(2,1)S(1)}, u32[]{:S(2)}, u32[]{:S(2)}) %collective-permute-start) | collective-permute-done | bytes 73760 | tf_op jit(solution)/shard_map/ppermute | solution.py:23
  7.9 0.7 select_dynamic-update-slice_fusion
  8.5 15.8 %all-to-all-start = ((bf16[16,32,1152]{2,1,0:T(8,128)(2,1)}), bf16[16,32,1152]{2,1,0:T(8,128)(2,1)}, u32[]{:S(2)}, u32[]{:S(2)}) async-start(bf16[16,32,1152]{2,1,0:T(8,128)(2,1)} %select_dynamic-update-slice_fusion), calls=%async_computation | async-start | bytes 2359296 | tf_op jit(solution)/shard_map/all_to_all | solution.py:156
  24.3 0.6 fusion.6
  24.9 1.3 %fusion.5 = s32[]{:T(128)} fusion(s32[256]{0:T(256)S(1)} %copy-done.4, s32[]{:T(128)} %fusion.6), kind=kLoop, calls=%fused_computation.11 | loop fusion | flops 767 | bytes 1032 | tf_op jit(solution)/shard_map/reduce_sum | solution.py:31
  26.9 0.0 copy-start.1
  26.9 1.7 %copy.12 = bf16[1152,576]{1,0:T(8,128)(2,1)} copy(bf16[1152,576]{0,1:T(8,128)(2,1)S(1)} %copy-done) | data formatting | bytes 2654208 | tf_op args[6]
  28.6 1.6 %copy.11 = bf16[1152,576]{1,0:T(8,128)(2,1)} copy(bf16[1152,576]{0,1:T(8,128)(2,1)S(1)} %copy-done.1) | data formatting | bytes 2654208 | tf_op args[7]
  30.2 0.2 cosine_add_fusion
  30.4 2.7 %pad_maximum_fusion.weight_ref = bf16[1152,1152]{1,0:T(8,128)(2,1)S(1)} fusion(bf16[1152,576]{1,0:T(8,128)(2,1)} %copy.12, bf16[1152,576]{1,0:T(8,128)(2,1)} %copy.11), kind=kLoop, calls=%fused_computation | loop fusion | flops 5308416 | bytes 5308416 | tf_op jit(solution)/shard_map/concatenate | solution.py:163
  33.1 9.4 %all-to-all-done = bf16[16,32,1152]{2,1,0:T(8,128)(2,1)} async-done(((bf16[16,32,1152]{2,1,0:T(8,128)(2,1)}), bf16[16,32,1152]{2,1,0:T(8,128)(2,1)}, u32[]{:S(2)}, u32[]{:S(2)}) %all-to-all-start) | async-done | bytes 1179680 | tf_op jit(solution)/shard_map/all_to_all | solution.py:156
  42.5 3.9 %project.1 = (bf16[512,1152]{1,0:T(8,128)(2,1)S(1)}, bf16[512,1152]{1,0:T(8,128)(2,1)S(1)}) custom-call(bf16[512,1152]{1,0:T(8,128)(2,1)} %bitcast.1.tokens_hbm, f32[1,1152]{1,0:T(1,128)S(1)} %get-tuple-element.7.stretch_ref, f32[1,1152]{1,0:T(1,128)S(1)} %get-tuple-element.6.offset_ref, bf16[1152,1152]{1,0:T(8,128)(2,1)S(1)} %pad_maximum_fusion.weight_ref), custom_call_target="tpu_custom_call" | custom-call | tf_op jit(solution)/shard_map/project/pallas_call | solution.py:74
  46.4 1.9 %collective-permute-start.1 = (bf16[512,1152]{1,0:T(8,128)(2,1)S(1)}, bf16[512,1152]{1,0:T(8,128)(2,1)S(1)}, u32[]{:S(2)}, u32[]{:S(2)}) collective-permute-start(bf16[512,1152]{1,0:T(8,128)(2,1)S(1)} %get-tuple-element.5.own_ref), channel_id=1, source_target_pairs={{0,1},{1,0},{2,3},{3,2},{4,5},{5,4},{6,7},{7,6},{8,9},{9,8},{10,11... | collective-permute-start | bytes 3538952 | tf_op jit(solution)/shard_map/ppermute | solution.py:165
  48.3 1.2 %fusion.2.query_ref = bf16[512,640]{1,0:T(8,128)(2,1)S(1)} fusion(bf16[512,1152]{1,0:T(8,128)(2,1)S(1)} %get-tuple-element.4, bf16[1152,576]{0,1:T(8,128)(2,1)S(1)} %copy-done.7), kind=kOutput, calls=%fused_computation.3 | convolution fusion | flops 755302400 | bytes 3162112 | tf_op jit(solution)/shard_map/dot_general | solution.py:167
  49.5 1.6 %collective-permute-done.1.other_ref = bf16[512,1152]{1,0:T(8,128)(2,1)S(1)} collective-permute-done((bf16[512,1152]{1,0:T(8,128)(2,1)S(1)}, bf16[512,1152]{1,0:T(8,128)(2,1)S(1)}, u32[]{:S(2)}, u32[]{:S(2)}) %collective-permute-start.1) | collective-permute-done | bytes 1179680 | tf_op jit(solution)/shard_map/ppermute | solution.py:165
  51.1 5.8 %attention.1 = bf16[512,576]{1,0:T(8,128)(2,1)S(1)} custom-call(bf16[512,640]{1,0:T(8,128)(2,1)S(1)} %fusion.2.query_ref, bf16[512,1152]{1,0:T(8,128)(2,1)S(1)} %get-tuple-element.5.own_ref, bf16[512,1152]{1,0:T(8,128)(2,1)S(1)} %collective-permute-done.1.other_ref), custom_call_target="tpu_custom_call" | custom-call | tf_op jit(solution)/shard_map/attention/pallas_call | solution.py:137
  56.9 31.3 %all_to_all.10 = bf16[16,32,576]{2,1,0:T(8,128)(2,1)S(1)} all-to-all(bf16[16,32,576]{2,1,0:T(8,128)(2,1)S(1)} %bitcast.5), channel_id=1, replica_groups={{20,22,16,26,28,0,18,14,12,30,2,6,4,24,8,10},{21,23,17,27,29,1,19,15,13..., dimensions={0} | all-to-all | bytes 1179648 | tf_op jit(solution)/shard_map/all_to_all | solution.py:169
  88.2 0.8 copy.15
  (14 shorter events, 0.0 us)
Async XLA Ops:
  0.6 4.5 %slice-start = ((bf16[16,32,1152]{2,1,0:T(8,128)(2,1)}), bf16[15,32,1152]{2,1,0:T(8,128)(2,1)S(1)}, s32[]{:S(2)}) async-start(bf16[16,32,1152]{2,1,0:T(8,128)(2,1)} %param.9), calls=%async_computation.2 | async-start | bytes 2211840 | tf_op jit(solution)/shard_map/slice | solution.py:154
  0.6 4.5 %copy-start.2 = (bf16[32,1152]{1,0:T(8,128)(2,1)S(1)}, bf16[32,1152]{1,0:T(8,128)(2,1)}, u32[]{:S(2)}) copy-start(bf16[32,1152]{1,0:T(8,128)(2,1)} %param.10) | copy-start | bytes 221188
  1.6 6.2 %collective-permute-start = (bf16[1,32,1152]{2,1,0:T(8,128)(2,1)S(1)}, bf16[1,32,1152]{2,1,0:T(8,128)(2,1)S(1)}, u32[]{:S(2)}, u32[]{:S(2)}) collective-permute-start(bf16[1,32,1152]{2,1,0:T(8,128)(2,1)S(1)} %slice.13), channel_id=1, source_target_pairs={{0,32},{32,64},{64,96},{96,128},{128,160},{160,192},{192,224},{224... | collective-permute-start | bytes 221192 | tf_op jit(solution)/shard_map/ppermute | solution.py:23
  6.3 18.0 %copy-start.5 = (s32[16]{0:T(128)S(1)}, s32[16]{0:T(128)}, u32[]{:S(2)}) copy-start(s32[16]{0:T(128)} %param.11) | copy-start | bytes 196
  6.3 18.0 %copy-start.6 = (s32[16]{0:T(128)S(1)}, s32[16]{0:T(128)}, u32[]{:S(2)}) copy-start(s32[16]{0:T(128)} %constant.35.clone) | copy-start | bytes 196
  6.3 18.7 %copy-start.4 = (s32[256]{0:T(256)S(1)}, s32[256]{0:T(256)}, u32[]{:S(2)}) copy-start(s32[256]{0:T(256)} %param.12) | copy-start | bytes 3076
  6.3 20.6 %copy-start = (bf16[1152,576]{0,1:T(8,128)(2,1)S(1)}, bf16[1152,576]{0,1:T(8,128)(2,1)}, u32[]{:S(2)}) copy-start(bf16[1152,576]{0,1:T(8,128)(2,1)} %param.15) | copy-start | bytes 3981316
  8.5 34.0 %all-to-all-start = ((bf16[16,32,1152]{2,1,0:T(8,128)(2,1)}), bf16[16,32,1152]{2,1,0:T(8,128)(2,1)}, u32[]{:S(2)}, u32[]{:S(2)}) async-start(bf16[16,32,1152]{2,1,0:T(8,128)(2,1)} %select_dynamic-update-slice_fusion), calls=%async_computation | async-start | bytes 2359296 | tf_op jit(solution)/shard_map/all_to_all | solution.py:156
  26.9 1.7 %copy-start.1 = (bf16[1152,576]{0,1:T(8,128)(2,1)S(1)}, bf16[1152,576]{0,1:T(8,128)(2,1)}, u32[]{:S(2)}) copy-start(bf16[1152,576]{0,1:T(8,128)(2,1)} %param.16) | copy-start | bytes 3981316
  28.6 1.7 %copy-start.3 = (f32[2,1152]{1,0:T(2,128)S(1)}, f32[2,1152]{1,0:T(2,128)}, u32[]{:S(2)}) copy-start(f32[2,1152]{1,0:T(2,128)} %param.13) | copy-start | bytes 27652
  42.5 5.8 %copy-start.7 = (bf16[1152,576]{0,1:T(8,128)(2,1)S(1)}, bf16[1152,576]{0,1:T(8,128)(2,1)}, u32[]{:S(2)}) copy-start(bf16[1152,576]{0,1:T(8,128)(2,1)} %param.14) | copy-start | bytes 3981316
  46.4 4.7 %collective-permute-start.1 = (bf16[512,1152]{1,0:T(8,128)(2,1)S(1)}, bf16[512,1152]{1,0:T(8,128)(2,1)S(1)}, u32[]{:S(2)}, u32[]{:S(2)}) collective-permute-start(bf16[512,1152]{1,0:T(8,128)(2,1)S(1)} %get-tuple-element.5.own_ref), channel_id=1, source_target_pairs={{0,1},{1,0},{2,3},{3,2},{4,5},{5,4},{6,7},{7,6},{8,9},{9,8},{10,11... | collective-permute-start | bytes 3538952 | tf_op jit(solution)/shard_map/ppermute | solution.py:165

commit v7 on v6

--- a/solution.py
+++ b/solution.py
@@ -11,6 +11,7 @@
 HEADS = 8
 HD = 72
 LANE = 128
+RUN = 16
 WIDTH = HEADS * HD
 SHIFT = WIDTH % LANE
 OWNERS = (10, 11, 8, 13, 14, 0, 9, 7, 6, 15, 1, 3, 2, 12, 4, 5)
@@ -88,7 +89,7 @@
     )(tokens, stretch, offset, weight)
 
 
-def attention_kernel(query_ref, own_ref, other_ref, out_ref):
+def attention_kernel(query_ref, own_ref, other_ref, out_ref, result_ref):
     dims = (((1,), (1,)), ((), ()))
     window = 2 * LANE
     rows = query_ref.shape[0]
@@ -123,12 +124,13 @@
             done = result
         else:
             if start != done_start:
-                out_ref[:, pl.ds(done_start, LANE)] = done[:, :LANE].astype(jnp.bfloat16)
+                result_ref[:, pl.ds(done_start, LANE)] = done[:, :LANE].astype(jnp.bfloat16)
                 done = jnp.concatenate([done[:, LANE:], result[:, LANE:]], axis=1)
             done = jnp.where(lane < first, done, result)
         done_start = start
-    tail = WIDTH - done_start
-    out_ref[:, pl.ds(done_start, tail)] = done[:, :tail].astype(jnp.bfloat16)
+    result_ref[:, pl.ds(done_start, window)] = done.astype(jnp.bfloat16)
+    runs = result_ref[...].reshape(-1, 2, RUN, result_ref.shape[1])[:, :, :, :WIDTH]
+    out_ref[...] = jnp.concatenate([runs[:, 0], runs[:, 1]], axis=-1)
 
 
 def attend(query, own, other):
@@ -136,9 +138,10 @@
     rows = query.shape[0]
     return pl.pallas_call(
         attention_kernel,
-        out_shape=jax.ShapeDtypeStruct((rows, WIDTH), jnp.bfloat16),
+        out_shape=jax.ShapeDtypeStruct((rows // (2 * RUN), RUN, 2 * WIDTH), jnp.bfloat16),
         in_specs=[vmem] * 3,
         out_specs=vmem,
+        scratch_shapes=[pltpu.VMEM((rows, pl.cdiv(WIDTH, LANE) * LANE), jnp.bfloat16)],
         compiler_params=pltpu.CompilerParams(vmem_limit_bytes=32 * 2**20),
         name="attention",
     )(query, own, other)
@@ -166,14 +169,10 @@
     w_shifted = jnp.pad(w_query, ((0, 0), (SHIFT, 0)))
     query = jnp.dot(normed, w_shifted, preferred_element_type=jnp.float32).astype(jnp.bfloat16)
     result = attend(query, own, other)
-    attended = lax.all_to_all(
-        result.reshape(frames, tokens_dev, WIDTH),
-        "tok",
-        split_axis=0,
-        concat_axis=0,
-        axis_index_groups=same_core,
-        tiled=True,
+    back = lax.all_to_all(
+        result, "tok", split_axis=0, concat_axis=0, axis_index_groups=same_core, tiled=True
     )
+    attended = jnp.concatenate([back[:, :, :WIDTH], back[:, :, WIDTH:]], axis=1)
     return (queued, attended)
 
 

time: 90.6 us -> 89.7 us (0.990)
  the two profiles are of different devices: /device:TPU:56 before, /device:TPU:96 now
where the time goes in v7:
time: 89.7 us; the launch traced here: 89.4 us
  blocking collectives  24.2 us (27%)
  waiting for transfers between devices  21.5 us (24%)
  starting transfers between devices  19.4 us (22%)
  Pallas kernels  9.77 us (11%)
  other arithmetic  7.5 us (8%)
  local copies, waits for them, and re-layouts  4.48 us (5%)
  between operations  1.38 us (2%)
  matrix products  1.18 us (1%)
    all_to_all x1, blocking collectives, shards(): lax.all_to_all(result, 'tok', split_axis=0, concat_axis=0, axis_index_gro...  24.2 us
    all_to_all x1, waiting for transfers between devices, shards(): lax.all_to_all(queued, 'tok', split_axis=0, concat_axis=0, axis_index_gro...  16.1 us
    all_to_all x1, starting transfers between devices, shards(): lax.all_to_all(queued, 'tok', split_axis=0, concat_axis=0, axis_index_gro...  14.9 us
    pallas_call x1, Pallas kernels, attend(): pl.pallas_call(attention_kernel, out_shape=jax.ShapeDtypeStruct((rows //...  5.89 us
    pallas_call x1, Pallas kernels, normalize_and_project(): pl.pallas_call(project_kernel, out_shape=(jax.ShapeDtypeStruct(tokens.sha...  3.88 us
    ppermute x1, waiting for transfers between devices, from_behind(): return lax.ppermute(block, axis, route)  3.7 us
    unnamed x18, local copies, waits for them, and re-layouts  3.34 us
    concatenate x1, other arithmetic, shards(): w_pair = jnp.concatenate([w_value, w_key], axis=1)  2.67 us
  transfers between devices with their start and end apart: 3, of which 3 were waited for; matrix products, arithmetic and copies ran while one was open for 12% of the time, Pallas kernels for 0%

profile of v7, /device:TPU:96, one launch (start us, length us, event | category | flops | bytes accessed | tf_op | source)
XLA Modules:
  0.0 89.4 jit_solution(11806054165631455787)
XLA Ops:
  0.6 0.0 slice-start
  0.6 1.0 %slice.19 = bf16[1,32,1152]{2,1,0:T(8,128)(2,1)S(1)} slice(bf16[16,32,1152]{2,1,0:T(8,128)(2,1)} %param.9), slice={[15:16], [0:32], [0:1152]} | slice | bytes 147456 | tf_op jit(solution)/shard_map/slice | solution.py:155
  1.6 2.6 %collective-permute-start = (bf16[1,32,1152]{2,1,0:T(8,128)(2,1)S(1)}, bf16[1,32,1152]{2,1,0:T(8,128)(2,1)S(1)}, u32[]{:S(2)}, u32[]{:S(2)}) collective-permute-start(bf16[1,32,1152]{2,1,0:T(8,128)(2,1)S(1)} %slice.19), channel_id=1, source_target_pairs={{0,32},{32,64},{64,96},{96,128},{128,160},{160,192},{192,224},{224... | collective-permute-start | bytes 221192 | tf_op jit(solution)/shard_map/ppermute | solution.py:24
  4.2 1.1 %pad_maximum_fusion.1 = bf16[16,32,1152]{2,1,0:T(8,128)(2,1)} fusion(bf16[15,32,1152]{2,1,0:T(8,128)(2,1)S(1)} %slice-done, bf16[1,32,1152]{2,1,0:T(8,128)(2,1)S(1)} %bitcast.4), kind=kLoop, calls=%fused_computation.4 | loop fusion | flops 589824 | bytes 2359296 | tf_op jit(solution)/shard_map/concatenate | solution.py:157
  5.4 3.7 %collective-permute-done = bf16[1,32,1152]{2,1,0:T(8,128)(2,1)S(1)} collective-permute-done((bf16[1,32,1152]{2,1,0:T(8,128)(2,1)S(1)}, bf16[1,32,1152]{2,1,0:T(8,128)(2,1)S(1)}, u32[]{:S(2)}, u32[]{:S(2)}) %collective-permute-start) | collective-permute-done | bytes 73760 | tf_op jit(solution)/shard_map/ppermute | solution.py:24
  9.1 0.7 select_dynamic-update-slice_fusion
  9.7 14.9 %all-to-all-start = ((bf16[16,32,1152]{2,1,0:T(8,128)(2,1)}), bf16[16,32,1152]{2,1,0:T(8,128)(2,1)}, u32[]{:S(2)}, u32[]{:S(2)}) async-start(bf16[16,32,1152]{2,1,0:T(8,128)(2,1)} %select_dynamic-update-slice_fusion), calls=%async_computation | async-start | bytes 2359296 | tf_op jit(solution)/shard_map/all_to_all | solution.py:159
  24.6 0.0 copy-done.5
  24.6 0.6 fusion.6
  25.3 1.3 %fusion.5 = s32[]{:T(128)} fusion(s32[256]{0:T(256)S(1)} %copy-done.4, s32[]{:T(128)} %fusion.6), kind=kLoop, calls=%fused_computation.12 | loop fusion | flops 767 | bytes 1032 | tf_op jit(solution)/shard_map/reduce_sum | solution.py:32
  27.2 0.0 copy-start.1
  27.2 1.7 %copy.12 = bf16[1152,576]{1,0:T(8,128)(2,1)} copy(bf16[1152,576]{0,1:T(8,128)(2,1)S(1)} %copy-done) | data formatting | bytes 2654208 | tf_op args[6]
  28.9 1.6 %copy.11 = bf16[1152,576]{1,0:T(8,128)(2,1)} copy(bf16[1152,576]{0,1:T(8,128)(2,1)S(1)} %copy-done.1) | data formatting | bytes 2654208 | tf_op args[7]
  30.6 0.2 cosine_add_fusion
  30.7 2.7 %pad_maximum_fusion.weight_ref = bf16[1152,1152]{1,0:T(8,128)(2,1)S(1)} fusion(bf16[1152,576]{1,0:T(8,128)(2,1)} %copy.12, bf16[1152,576]{1,0:T(8,128)(2,1)} %copy.11), kind=kLoop, calls=%fused_computation | loop fusion | flops 5308416 | bytes 5308416 | tf_op jit(solution)/shard_map/concatenate | solution.py:166
  33.4 16.1 %all-to-all-done = bf16[16,32,1152]{2,1,0:T(8,128)(2,1)} async-done(((bf16[16,32,1152]{2,1,0:T(8,128)(2,1)}), bf16[16,32,1152]{2,1,0:T(8,128)(2,1)}, u32[]{:S(2)}, u32[]{:S(2)}) %all-to-all-start) | async-done | bytes 1179680 | tf_op jit(solution)/shard_map/all_to_all | solution.py:159
  49.6 3.9 %project.1 = (bf16[512,1152]{1,0:T(8,128)(2,1)S(1)}, bf16[512,1152]{1,0:T(8,128)(2,1)S(1)}) custom-call(bf16[512,1152]{1,0:T(8,128)(2,1)} %bitcast.1.tokens_hbm, f32[1,1152]{1,0:T(1,128)S(1)} %get-tuple-element.9.stretch_ref, f32[1,1152]{1,0:T(1,128)S(1)} %get-tuple-element.8.offset_ref, bf16[1152,1152]{1,0:T(8,128)(2,1)S(1)} %pad_maximum_fusion.weight_ref), custom_call_target="tpu_custom_call" | custom-call | tf_op jit(solution)/shard_map/project/pallas_call | solution.py:75
  53.4 1.9 %collective-permute-start.1 = (bf16[512,1152]{1,0:T(8,128)(2,1)S(1)}, bf16[512,1152]{1,0:T(8,128)(2,1)S(1)}, u32[]{:S(2)}, u32[]{:S(2)}) collective-permute-start(bf16[512,1152]{1,0:T(8,128)(2,1)S(1)} %get-tuple-element.5.own_ref), channel_id=1, source_target_pairs={{0,1},{1,0},{2,3},{3,2},{4,5},{5,4},{6,7},{7,6},{8,9},{9,8},{10,11... | collective-permute-start | bytes 3538952 | tf_op jit(solution)/shard_map/ppermute | solution.py:168
  55.4 1.2 %fusion.2.query_ref = bf16[512,640]{1,0:T(8,128)(2,1)S(1)} fusion(bf16[512,1152]{1,0:T(8,128)(2,1)S(1)} %get-tuple-element.4, bf16[1152,576]{0,1:T(8,128)(2,1)S(1)} %copy-done.7), kind=kOutput, calls=%fused_computation.3 | convolution fusion | flops 755302400 | bytes 3162112 | tf_op jit(solution)/shard_map/dot_general | solution.py:170
  56.6 1.6 %collective-permute-done.1.other_ref = bf16[512,1152]{1,0:T(8,128)(2,1)S(1)} collective-permute-done((bf16[512,1152]{1,0:T(8,128)(2,1)S(1)}, bf16[512,1152]{1,0:T(8,128)(2,1)S(1)}, u32[]{:S(2)}, u32[]{:S(2)}) %collective-permute-start.1) | collective-permute-done | bytes 1179680 | tf_op jit(solution)/shard_map/ppermute | solution.py:168
  58.2 5.9 %attention.1 = bf16[16,16,1152]{2,1,0:T(8,128)(2,1)S(1)} custom-call(bf16[512,640]{1,0:T(8,128)(2,1)S(1)} %fusion.2.query_ref, bf16[512,1152]{1,0:T(8,128)(2,1)S(1)} %get-tuple-element.5.own_ref, bf16[512,1152]{1,0:T(8,128)(2,1)S(1)} %collective-permute-done.1.other_ref), custom_call_target="tpu_custom_call" | custom-call | tf_op jit(solution)/shard_map/attention/pallas_call | solution.py:139
  64.1 24.2 %all_to_all.10 = bf16[16,16,1152]{2,1,0:T(8,128)(2,1)S(1)} all-to-all(bf16[16,16,1152]{2,1,0:T(8,128)(2,1)S(1)} %attention.1), channel_id=1, replica_groups={{20,22,16,26,28,0,18,14,12,30,2,6,4,24,8,10},{21,23,17,27,29,1,19,15,13..., dimensions={0} | all-to-all | bytes 1179648 | tf_op jit(solution)/shard_map/all_to_all | solution.py:172
  88.3 0.2 fusion.8
  88.5 0.9 %pad_maximum_fusion.2 = bf16[16,32,576]{2,1,0:T(8,128)(2,1)} fusion(bf16[16,16,576]{2,1,0:T(8,128)(2,1)S(1)} %get-tuple-element.7, bf16[16,16,576]{2,1,0:T(8,128)(2,1)S(1)} %get-tuple-element.6), kind=kLoop, calls=%fused_computation.5 | loop fusion | flops 1179648 | bytes 1179648 | tf_op jit(solution)/shard_map/concatenate | solution.py:175
  (15 shorter events, 0.0 us)
Async XLA Ops:
  0.6 3.6 %slice-start = ((bf16[16,32,1152]{2,1,0:T(8,128)(2,1)}), bf16[15,32,1152]{2,1,0:T(8,128)(2,1)S(1)}, s32[]{:S(2)}) async-start(bf16[16,32,1152]{2,1,0:T(8,128)(2,1)} %param.9), calls=%async_computation.2 | async-start | bytes 2211840 | tf_op jit(solution)/shard_map/slice | solution.py:157
  0.6 3.6 %copy-start.2 = (bf16[32,1152]{1,0:T(8,128)(2,1)S(1)}, bf16[32,1152]{1,0:T(8,128)(2,1)}, u32[]{:S(2)}) copy-start(bf16[32,1152]{1,0:T(8,128)(2,1)} %param.10) | copy-start | bytes 221188
  1.6 7.4 %collective-permute-start = (bf16[1,32,1152]{2,1,0:T(8,128)(2,1)S(1)}, bf16[1,32,1152]{2,1,0:T(8,128)(2,1)S(1)}, u32[]{:S(2)}, u32[]{:S(2)}) collective-permute-start(bf16[1,32,1152]{2,1,0:T(8,128)(2,1)S(1)} %slice.19), channel_id=1, source_target_pairs={{0,32},{32,64},{64,96},{96,128},{128,160},{160,192},{192,224},{224... | collective-permute-start | bytes 221192 | tf_op jit(solution)/shard_map/ppermute | solution.py:24
  5.4 19.2 %copy-start.5 = (s32[16]{0:T(128)S(1)}, s32[16]{0:T(128)}, u32[]{:S(2)}) copy-start(s32[16]{0:T(128)} %param.11) | copy-start | bytes 196
  5.4 19.2 %copy-start.6 = (s32[16]{0:T(128)S(1)}, s32[16]{0:T(128)}, u32[]{:S(2)}) copy-start(s32[16]{0:T(128)} %constant.35.clone) | copy-start | bytes 196
  5.4 19.9 %copy-start.4 = (s32[256]{0:T(256)S(1)}, s32[256]{0:T(256)}, u32[]{:S(2)}) copy-start(s32[256]{0:T(256)} %param.12) | copy-start | bytes 3076
  5.4 21.9 %copy-start = (bf16[1152,576]{0,1:T(8,128)(2,1)S(1)}, bf16[1152,576]{0,1:T(8,128)(2,1)}, u32[]{:S(2)}) copy-start(bf16[1152,576]{0,1:T(8,128)(2,1)} %param.15) | copy-start | bytes 3981316
  9.7 39.8 %all-to-all-start = ((bf16[16,32,1152]{2,1,0:T(8,128)(2,1)}), bf16[16,32,1152]{2,1,0:T(8,128)(2,1)}, u32[]{:S(2)}, u32[]{:S(2)}) async-start(bf16[16,32,1152]{2,1,0:T(8,128)(2,1)} %select_dynamic-update-slice_fusion), calls=%async_computation | async-start | bytes 2359296 | tf_op jit(solution)/shard_map/all_to_all | solution.py:159
  27.2 1.7 %copy-start.1 = (bf16[1152,576]{0,1:T(8,128)(2,1)S(1)}, bf16[1152,576]{0,1:T(8,128)(2,1)}, u32[]{:S(2)}) copy-start(bf16[1152,576]{0,1:T(8,128)(2,1)} %param.16) | copy-start | bytes 3981316
  28.9 1.6 %copy-start.3 = (f32[2,1152]{1,0:T(2,128)S(1)}, f32[2,1152]{1,0:T(2,128)}, u32[]{:S(2)}) copy-start(f32[2,1152]{1,0:T(2,128)} %param.13) | copy-start | bytes 27652
  49.6 5.8 %copy-start.7 = (bf16[1152,576]{0,1:T(8,128)(2,1)S(1)}, bf16[1152,576]{0,1:T(8,128)(2,1)}, u32[]{:S(2)}) copy-start(bf16[1152,576]{0,1:T(8,128)(2,1)} %param.14) | copy-start | bytes 3981316
  53.4 4.7 %collective-permute-start.1 = (bf16[512,1152]{1,0:T(8,128)(2,1)S(1)}, bf16[512,1152]{1,0:T(8,128)(2,1)S(1)}, u32[]{:S(2)}, u32[]{:S(2)}) collective-permute-start(bf16[512,1152]{1,0:T(8,128)(2,1)S(1)} %get-tuple-element.5.own_ref), channel_id=1, source_target_pairs={{0,1},{1,0},{2,3},{3,2},{4,5},{5,4},{6,7},{7,6},{8,9},{9,8},{10,11... | collective-permute-start | bytes 3538952 | tf_op jit(solution)/shard_map/ppermute | solution.py:168
